TPU v7x, 512 devices: a whole 4x4x16 slice. The times are simulated.
512 devices in a mesh: ctx: 64 (over x, z), head: 8 (over y, core).
Axes of the slice: x: 4, y: 4, z: 16, core: 2. Of those that a mesh axis runs over, the one named last changes fastest.
Arguments:
- queries: bfloat16 [65536, 2048], P('ctx', 'head'), may hold values from -6 to 6
- lin_keys: bfloat16 [65536, 2048], P('ctx', 'head'), may hold values from -6 to 6
- lin_values: bfloat16 [65536, 2048], P('ctx', 'head'), may hold values from -6 to 6
- level_class: int32 [65536], P('ctx'), may hold values from 0 to 15
- level_table: float32 [16, 16, 11], P(None, 'head'), may hold values from 0.25 to 4
- win_keys: bfloat16 [65536, 512], P(('ctx', 'head')), may hold values from -6 to 6
- win_values: bfloat16 [65536, 512], P(('ctx', 'head')), may hold values from -6 to 6
- seg_ids: int32 [65536], P(('ctx', 'head')), may hold values from 0 to 255, never falling along the last dimension, each value on 1 to 2048 neighbouring positions
Outputs:
- mixed_heads: bfloat16 [65536, 2048], P('ctx', 'head')
- window_out: bfloat16 [65536, 2048], P(('ctx', 'head'))
Inputs may be any that keep to these rules, and one draw needn't show every extreme that they name: `seg_ids`: document numbers never fall along the tokens; each document has 1 to 2048 tokens and one has exactly 2048.
All inputs are finite; a program needn't handle non-finite values.
Results may differ from a plain program's by a relative error of at most 0.0085.
Values may be sent and summed in bfloat16 or wider, within the bound.
No kernel may reach another device: no remote copies, remote signals or barrier semaphores. Data moves between devices by JAX's collectives and lax.ppermute only.
A program may use at most 128 MiB of HBM per device.

v0:
```python
import jax
import jax.numpy as jnp
from jax import lax
from jax.sharding import PartitionSpec as P

H = 16
E = 128
KVH = 4
BLK = 64
W = 256
NCLASS = 16


HIGHEST_PREC = lax.Precision.HIGHEST


def from_behind(value, axis, by):
    size = lax.axis_size(axis)
    pairs = [(i, i + by) for i in range(size) if 0 <= i + by < size]
    return lax.ppermute(value, axis, pairs)


def top_bit(values, width):
    counted = jnp.zeros(values.shape, jnp.int32)
    for bit_num in range(width):
        counted = counted + (values >= 1 << bit_num).astype(jnp.int32)
    return counted


def softmax_rows(scores, allowed):
    row_max = jnp.max(jnp.where(allowed, scores, -jnp.inf), axis=-1, keepdims=True)
    exp_scores = jnp.exp(jnp.where(allowed, scores - row_max, -jnp.inf))
    return (exp_scores / jnp.sum(exp_scores, axis=-1, keepdims=True)).astype(jnp.bfloat16)


def local(queries, lin_keys, lin_values, level_class, level_table, win_keys, win_values, seg_ids):
    tok_rows = queries.shape[0]
    heads_here = queries.shape[1] // E
    levels = level_table.shape[2]
    span_bits = (tok_rows // BLK).bit_length() - 1
    local_levels = span_bits + 1
    ctx_bits = lax.axis_size("ctx").bit_length() - 1
    my_span = lax.axis_index("ctx")
    head_count = lax.axis_size("head")
    q_feats = (
        (1.0 + jax.nn.elu(queries.astype(jnp.float32)))
        .astype(jnp.bfloat16)
        .reshape(tok_rows, heads_here, E)
    )
    k_feats = (
        (1.0 + jax.nn.elu(lin_keys.astype(jnp.float32)))
        .astype(jnp.bfloat16)
        .reshape(tok_rows, heads_here, E)
    )
    v_heads = lin_values.reshape(tok_rows, heads_here, E)
    own_state = jnp.einsum("sha,shb->hab", k_feats, v_heads, preferred_element_type=jnp.float32)
    own_sum = jnp.sum(k_feats, axis=0, dtype=jnp.float32)
    level_ids = jnp.arange(ctx_bits, dtype=jnp.int32)
    zero_acc = (
        jnp.zeros((ctx_bits, heads_here, E, E), jnp.float32),
        jnp.zeros((ctx_bits, heads_here, E), jnp.float32),
    )
    piece_state = lax.all_gather(
        own_state[None].astype(jnp.bfloat16), "ctx", axis=0, tiled=True
    ).astype(jnp.float32)
    piece_sum = lax.all_gather(
        own_sum[None].astype(jnp.bfloat16), "ctx", axis=0, tiled=True
    ).astype(jnp.float32)
    others = jnp.arange(piece_state.shape[0], dtype=jnp.int32)
    pair_level = top_bit(jnp.bitwise_xor(others, my_span), ctx_bits) - 1
    picked = ((pair_level[:, None] == level_ids[None, :]) & (others < my_span)[:, None]).astype(
        jnp.float32
    )
    new_state = zero_acc[0] + jnp.einsum(
        "jl,jhab->lhab", picked, piece_state, precision=HIGHEST_PREC
    )
    new_sum = zero_acc[1] + jnp.einsum("jl,jha->lha", picked, piece_sum, precision=HIGHEST_PREC)
    class_hot = jax.nn.one_hot(level_class, NCLASS, dtype=jnp.float32)
    level_weight = jnp.dot(
        class_hot, level_table.reshape(NCLASS, heads_here * levels), precision=HIGHEST_PREC
    ).reshape(tok_rows, heads_here, levels)
    rows_blk = min(512, tok_rows)
    tok_ids = jnp.arange(tok_rows, dtype=jnp.int32)
    mixed_parts = []
    for first_row in range(0, tok_rows, rows_blk):
        row_ids = tok_ids[first_row : first_row + rows_blk]
        q_blk = q_feats[first_row : first_row + rows_blk]
        q_wide = q_blk.astype(jnp.float32)
        inner_level = top_bit(
            jnp.bitwise_xor(row_ids[:, None] // BLK, tok_ids[None, :] // BLK), span_bits
        )
        scores = jnp.einsum("tha,sha->hts", q_blk, k_feats, preferred_element_type=jnp.float32)
        scores = jnp.where((tok_ids[None, :] <= row_ids[:, None])[None], scores, 0.0)
        inner_den = jnp.stack(
            [
                jnp.sum(jnp.where(inner_level == level_num, scores, 0.0), axis=-1)
                for level_num in range(local_levels)
            ],
            axis=-1,
        )
        outer_den = jnp.einsum("tha,lha->htl", q_wide, new_sum, precision=HIGHEST_PREC)
        weight_rows = jnp.transpose(level_weight[first_row : first_row + rows_blk], (1, 0, 2))
        coeffs = weight_rows / jnp.maximum(jnp.concatenate([inner_den, outer_den], axis=-1), 1.0)
        weight = jnp.zeros(scores.shape, jnp.float32)
        for level_num in range(local_levels):
            weight = weight + jnp.where(
                inner_level == level_num, coeffs[:, :, level_num : level_num + 1], 0.0
            )
        weight = (weight * scores).astype(jnp.bfloat16)
        inner_part = jnp.einsum("hts,shb->thb", weight, v_heads, preferred_element_type=jnp.float32)
        through = jnp.einsum("tha,lhab->htlb", q_wide, new_state, precision=HIGHEST_PREC)
        outer_part = jnp.einsum(
            "htlb,htl->thb", through, coeffs[:, :, local_levels:], precision=HIGHEST_PREC
        )
        mixed_parts.append(
            (inner_part + outer_part).astype(jnp.bfloat16).reshape(rows_blk, heads_here * E)
        )
    mixed_heads = jnp.concatenate(mixed_parts, axis=0)
    group_size = H // KVH
    score_scale = E ** (-0.5)
    gate_scale = 0.5 + jax.nn.sigmoid(mixed_heads.astype(jnp.float32))
    queries_gated = (queries.astype(jnp.float32) * gate_scale).astype(jnp.bfloat16)
    token_queries = lax.all_to_all(queries_gated, "head", split_axis=0, concat_axis=1, tiled=True)
    tok_here = token_queries.shape[0]
    steps_back = (W + tok_here - 2) // tok_here
    rim_parts = [
        from_behind((win_keys, win_values, seg_ids), ("ctx", "head"), distance)
        for distance in range(steps_back, 0, -1)
    ]
    keys_all = jnp.concatenate([rim_piece[0] for rim_piece in rim_parts] + [win_keys], axis=0)
    values_all = jnp.concatenate([rim_piece[1] for rim_piece in rim_parts] + [win_values], axis=0)
    segs_all = jnp.concatenate([rim_piece[2] for rim_piece in rim_parts] + [seg_ids], axis=0)
    first_pos = (my_span * head_count + lax.axis_index("head")) * tok_here
    q_pos = first_pos + jnp.arange(tok_here, dtype=jnp.int32)
    k_pos = (
        first_pos - steps_back * tok_here + jnp.arange((steps_back + 1) * tok_here, dtype=jnp.int32)
    )
    allowed = (
        (k_pos[None, :] <= q_pos[:, None])
        & (k_pos[None, :] > q_pos[:, None] - W)
        & (k_pos[None, :] >= 0)
        & (segs_all[None, :] == seg_ids[:, None])
    )
    scores = (
        jnp.einsum(
            "tkga,ska->kgts",
            token_queries.reshape(tok_here, KVH, group_size, E),
            keys_all.reshape(-1, KVH, E),
            preferred_element_type=jnp.float32,
        )
        * score_scale
    )
    weights_bf = softmax_rows(scores, allowed)
    out_rows = jnp.einsum(
        "kgts,skb->tkgb",
        weights_bf,
        values_all.reshape(-1, KVH, E),
        preferred_element_type=jnp.float32,
    )
    window_out = out_rows.reshape(tok_here, H * E).astype(jnp.bfloat16)
    return (mixed_heads, window_out)


def solution(mesh):
    return jax.shard_map(
        local,
        mesh=mesh,
        in_specs=(
            P("ctx", "head"),
            P("ctx", "head"),
            P("ctx", "head"),
            P("ctx"),
            P(None, "head", None),
            P(("ctx", "head"), None),
            P(("ctx", "head"), None),
            P(("ctx", "head")),
        ),
        out_specs=(P("ctx", "head"), P(("ctx", "head"), None)),
        check_vma=False,
    )
```

profile of v0, /device:TPU:1, one launch (start us, length us, event | category | flops | bytes accessed | tf_op | source)
XLA Modules:
  0.0 215.6 jit_solution(6930815832092844440)
XLA Ops:
  7.2 1.3 copy.75
  8.6 0.6 fusion.68
  9.2 0.8 copy-done.16
  9.9 0.9 convolution_convert_fusion
  10.9 4.6 %collective-permute-start.3 = (s32[128]{0:T(128)}, s32[128]{0:T(128)}, u32[]{:S(2)}, u32[]{:S(2)}) collective-permute-start(s32[128]{0:T(128)} %param.15), channel_id=1, source_target_pairs={{0,1},{1,2},{2,3},{3,4},{4,5},{5,6},{6,7},{7,8},{8,9},{9,10},{10,1... | collective-permute-start | bytes 1544 | tf_op jit(solution)/shard_map/ppermute | solution.py:20
  15.5 3.7 %collective-permute-start.2 = (s32[128]{0:T(128)}, s32[128]{0:T(128)}, u32[]{:S(2)}, u32[]{:S(2)}) collective-permute-start(s32[128]{0:T(128)} %param.15), channel_id=1, source_target_pairs={{0,2},{1,3},{2,4},{3,5},{4,6},{5,7},{6,8},{7,9},{8,10},{9,11},{10,... | collective-permute-start | bytes 1544 | tf_op jit(solution)/shard_map/ppermute | solution.py:20
  19.2 1.0 copy.92
  20.2 1.9 collective-permute-start.5
  22.2 3.3 %collective-permute-start.4 = (bf16[128,512]{0,1:T(8,128)(2,1)S(1)}, bf16[128,512]{0,1:T(8,128)(2,1)}, u32[]{:S(2)}, u32[]{:S(2)}) collective-permute-start(bf16[128,512]{0,1:T(8,128)(2,1)S(1)} %copy.92), channel_id=1, source_target_pairs={{0,2},{1,3},{2,4},{3,5},{4,6},{5,7},{6,8},{7,9},{8,10},{9,11},{10,... | collective-permute-start | bytes 393224 | tf_op jit(solution)/shard_map/ppermute | solution.py:20
  25.5 3.2 %collective-permute-start = (bf16[128,512]{1,0:T(8,128)(2,1)}, bf16[128,512]{1,0:T(8,128)(2,1)}, u32[]{:S(2)}, u32[]{:S(2)}) collective-permute-start(bf16[128,512]{1,0:T(8,128)(2,1)} %param.14), channel_id=1, source_target_pairs={{0,2},{1,3},{2,4},{3,5},{4,6},{5,7},{6,8},{7,9},{8,10},{9,11},{10,... | collective-permute-start | bytes 393224 | tf_op jit(solution)/shard_map/ppermute | solution.py:20
  28.7 0.8 copy.73
  29.6 1.2 fusion.33
  31.1 0.4 iota_compare_fusion.1
  31.5 0.5 fusion.23
  32.0 5.6 %broadcast_compare_fusion.3 = (pred[512,1024]{1,0:T(8,128)(4,1)S(1)}, pred[512,1024]{1,0:T(8,128)(4,1)S(1)}, pred[512,1024]{1,0:T(8,128)(4,1)S(1)}, pred[512,102...) fusion(s32[1024]{0:T(1024)S(1)} %add_select_fusion, ...), kind=kLoop, calls=%fused_computation.65 | loop fusion | flops 17825792 | bytes 5251072 | tf_op jit(solution)/shard_map/eq | solution.py:107
  37.6 5.6 %select_reduce_fusion.5 = (f32[2,512]{1,0:T(2,128)S(1)}, f32[2,512]{1,0:T(2,128)S(1)}, f32[2,512]{1,0:T(2,128)S(1)}, f32[2,512]{1,0:T(2,128)S(1)}, f32[2,512]{1,0:T(2,128)S(1)}, /*index=5*/f32[2,512,1024]{2,1,0:T(8,128)}) fusion(pred[512,1024]{1,0:T(8,128)(4,1)S(1)} %get-tuple-element.40, pred[512,1024]{1,0:T(8,128)(4,1)S(1)} %iota_compare_fusion.1, ...), kind=kOutput, calls=%fused_computation.18 | convolution fusion | flops 279964672 | bytes 8146944 | tf_op jit(solution)/shard_map/tha,sha->hts/dot_general | solution.py:92
  43.3 70.3 %all_gather.6 = bf16[64,2,128]{2,1,0:T(2,128)(2,1)S(1)} all-gather(bf16[1,2,128]{2,1,0:T(2,128)(2,1)S(1)} %bitcast.178), channel_id=1, replica_groups=mesh['ctx'=64,'head'=8] {'ctx'}, dimensions={0}, use_global_device_ids=true | all-gather | bytes 33280 | tf_op jit(solution)/shard_map/all_gather | solution.py:66
  113.8 0.2 fusion.77
  114.0 0.2 copy-done.23
  114.5 0.6 copy.186
  115.1 0.6 copy.187
  115.7 0.6 copy.188
  116.2 0.6 copy.189
  116.8 0.4 iota_compare_fusion
  117.2 7.0 %select_reduce_fusion = (f32[2,512]{1,0:T(2,128)S(1)}, f32[2,512]{1,0:T(2,128)S(1)}, f32[2,512]{1,0:T(2,128)S(1)}, f32[2,512]{1,0:T(2,128)S(1)}, f32[2,512]{1,0:T(2,128)S(1)}, /*index=5*/f32[2,512,1024]{2,1,0:T(8,128)}) fusion(pred[512,1024]{1,0:T(8,128)(4,1)S(1)} %get-tuple-element.46, pred[512,1024]{1,0:T(8,128)(4,1)S(1)} %iota_compare_fusion, ...), kind=kOutput, calls=%fused_computation.12 | convolution fusion | flops 279964672 | bytes 8146944 | tf_op jit(solution)/shard_map/tha,sha->hts/dot_general | solution.py:92
  124.7 0.5 broadcast_compare_fusion.10
  125.2 0.6 iota_add_fusion.1
  126.0 12.2 %collective-permute-start.1 = (bf16[128,512]{1,0:T(8,128)(2,1)}, bf16[128,512]{1,0:T(8,128)(2,1)S(1)}, u32[]{:S(2)}, u32[]{:S(2)}) collective-permute-start(bf16[128,512]{1,0:T(8,128)(2,1)} %param.14), channel_id=1, source_target_pairs={{0,1},{1,2},{2,3},{3,4},{4,5},{5,6},{6,7},{7,8},{8,9},{9,10},{10,1... | collective-permute-start | bytes 393224 | tf_op jit(solution)/shard_map/ppermute | solution.py:20
  138.2 0.7 pad_add_fusion
  138.8 15.4 %all-gather.3.cloned.1.call-done = bf16[128,128,128]{2,1,0:T(8,128)(2,1)} async-done(((bf16[2,128,128]{2,1,0:T(8,128)(2,1)}), bf16[128,128,128]{2,1,0:T(8,128)(2,1)}) %all-gather.3.cloned.1.call-update) | async-done | bytes 4194320 | tf_op jit(solution)/shard_map/all_gather | solution.py:63
  154.3 4.5 %fusion.1 = f32[6,2,128,128]{3,0,2,1:T(8,128)S(1)} fusion(bf16[64,2,128,128]{3,2,1,0:T(8,128)(2,1)} %bitcast.150, s32[64]{0:T(128)} %copy-done.24, pred[64]{0:T(512)(128)(4,1)} %copy-done.23), kind=kOutput, calls=%fused_computation.9 | convolution fusion | flops 25166592 | bytes 4981056 | tf_op jit(solution)/shard_map/jl,jhab->lhab/dot_general | solution.py:74
  158.8 2.6 %multiply_reduce_fusion.1 = f32[512,2,128]{2,0,1:T(8,128)} fusion(bf16[512,2,128,1]{0,2,3,1:T(8,128)(2,1)S(1)} %bitcast.156, f32[512,2,6]{0,2,1:T(8,128)S(1)} %slice_bitcast_fusion.1, f32[6,2,128,128]{3,0,2,1:T(8,128)S(1)} %fusion.1), kind=kOutput, calls=%fused_computation.32 | convolution fusion | flops 1209401344 | bytes 1597440 | tf_op jit(solution)/shard_map/tha,lhab->htlb/dot_general | solution.py:111
  161.4 2.1 copy.113
  163.5 2.6 %multiply_reduce_fusion = f32[512,2,128]{2,0,1:T(8,128)} fusion(bf16[512,2,128,1]{0,2,3,1:T(8,128)(2,1)S(1)} %bitcast.153, f32[512,2,6]{0,2,1:T(8,128)S(1)} %slice_bitcast_fusion, f32[6,2,128,128]{3,0,2,1:T(8,128)S(1)} %fusion.1), kind=kOutput, calls=%fused_computation.31 | convolution fusion | flops 1209401344 | bytes 1597440 | tf_op jit(solution)/shard_map/tha,lhab->htlb/dot_general | solution.py:111
  166.0 1.2 copy.125
  167.4 6.5 %fusion.19 = bf16[512,2,128]{0,2,1:T(8,128)(2,1)S(1)} fusion(f32[512,2,128]{0,2,1:T(8,128)} %copy.113, f32[2,512,1024]{2,1,0:T(8,128)} %get-tuple-element.56, f32[2,512]{1,0:T(2,128)S(1)} %bitcast.169, f32[2,512]{1,0:T(2,128)S(1)} %bitcast.170, f32[2,512]{1,0:T(2,128)S(1)} %bitcast.171, f32[2,512]{1,0:T(2,128)S(1)} %bitcast.172, ...), kind=kOutput, calls=%fused_computation.53 | convolution fusion | flops 281280512 | bytes 8671232 | tf_op jit(solution)/shard_map/hts,shb->thb/dot_general | solution.py:110
  174.0 4.1 %fusion.18 = bf16[512,2,128]{0,2,1:T(8,128)(2,1)S(1)} fusion(f32[512,2,128]{0,2,1:T(8,128)S(1)} %copy.125, f32[2,512,1024]{2,1,0:T(8,128)S(1)} %copy-done.29, f32[2,512]{1,0:T(2,128)S(1)} %bitcast.174, f32[2,512]{1,0:T(2,128)S(1)} %bitcast.175, f32[2,512]{1,0:T(2,128)S(1)} %bitcast.176, f32[2,512]{1,0:T(2,128)S(1)} %bitcast.177, ...), kind=kOutput, calls=%fused_computation.52 | convolution fusion | flops 281280512 | bytes 8671232 | tf_op jit(solution)/shard_map/hts,shb->thb/dot_general | solution.py:110
  178.1 1.1 copy_bitcast_fusion
  179.2 13.6 %all-to-all-start = ((bf16[8,128,256]{1,2,0:T(8,128)(2,1)}), bf16[8,128,256]{1,2,0:T(8,128)(2,1)S(1)}, u32[]{:S(2)}, u32[]{:S(2)}) async-start(bf16[8,128,256]{1,2,0:T(8,128)(2,1)} %copy_bitcast_fusion), calls=%async_computation | async-start | bytes 1048576 | tf_op jit(solution)/shard_map/all_to_all | solution.py:123
  192.9 0.2 compare_and_fusion
  193.2 0.9 pad_maximum_fusion.1
  194.1 0.2 copy.91
  194.3 1.0 pad_maximum_fusion.2
  195.4 1.0 copy.99
  196.4 5.9 %all-to-all-done = bf16[8,128,256]{1,2,0:T(8,128)(2,1)S(1)} async-done(((bf16[8,128,256]{1,2,0:T(8,128)(2,1)}), bf16[8,128,256]{1,2,0:T(8,128)(2,1)S(1)}, u32[]{:S(2)}, u32[]{:S(2)}) %all-to-all-start) | async-done | bytes 524320 | tf_op jit(solution)/shard_map/all_to_all | solution.py:123
  202.4 3.1 %fusion.76 = (f32[4,4,128]{2,1,0:T(4,128)S(1)}, f32[4,4,128,384]{2,3,1,0:T(8,128)}) fusion(pred[128,384]{0,1:T(8,128)(4,1)S(1)} %compare_and_fusion, bf16[384,4,128,1]{0,2,3,1:T(8,128)(2,1)S(1)} %bitcast.167, bf16[128,4,4,128]{0,3,2,1:T(8,128)(2,1)S(1)} %bitcast.161), kind=kOutput, calls=%fused_computation.164 | convolution fusion | flops 407372160 | bytes 4120576 | tf_op jit(solution)/shard_map/sub | solution.py:32
  205.4 2.3 %fusion.13 = bf16[4,128,4,128]{3,1,2,0:T(8,128)(2,1)S(1)} fusion(bf16[384,4,128,1]{0,2,3,1:T(8,128)(2,1)S(1)} %bitcast.166, f32[4,4,128,384]{2,3,1,0:T(8,128)} %get-tuple-element.58, f32[4,4,128]{2,1,0:T(4,128)S(1)} %get-tuple-element.57), kind=kOutput, calls=%fused_computation.47 | convolution fusion | flops 203161600 | bytes 4071424 | tf_op jit(solution)/shard_map/kgts,skb->tkgb/dot_general | solution.py:154
  207.8 1.0 copy.100
  (106 shorter events, 1.4 us)
Async XLA Ops:
  7.2 2.8 %copy-start = (bf16[1024,256]{1,0:T(8,128)(2,1)S(1)}, bf16[1024,256]{1,0:T(8,128)(2,1)}, u32[]{:S(2)}) copy-start(bf16[1024,256]{1,0:T(8,128)(2,1)} %param.10) | copy-start | bytes 1572868
  7.2 23.6 %copy-start.12 = (bf16[1024,256]{1,0:T(8,128)(2,1)S(1)}, bf16[1024,256]{1,0:T(8,128)(2,1)}, u32[]{:S(2)}) copy-start(bf16[1024,256]{1,0:T(8,128)(2,1)} %param.8) | copy-start | bytes 1572868
  7.2 147.1 %all-gather.3.cloned.1.call-start = ((), (), s32[]{:S(2)}) async-start(), calls=%async_computation.1 | async-start | bytes 4259840 | tf_op jit(solution)/shard_map/all_gather | solution.py:63
  9.2 0.8 copy-start.16
  10.9 115.1 %collective-permute-start.3 = (s32[128]{0:T(128)}, s32[128]{0:T(128)}, u32[]{:S(2)}, u32[]{:S(2)}) collective-permute-start(s32[128]{0:T(128)} %param.15), channel_id=1, source_target_pairs={{0,1},{1,2},{2,3},{3,4},{4,5},{5,6},{6,7},{7,8},{8,9},{9,10},{10,1... | collective-permute-start | bytes 1544 | tf_op jit(solution)/shard_map/ppermute | solution.py:20
  15.5 122.7 %collective-permute-start.2 = (s32[128]{0:T(128)}, s32[128]{0:T(128)}, u32[]{:S(2)}, u32[]{:S(2)}) collective-permute-start(s32[128]{0:T(128)} %param.15), channel_id=1, source_target_pairs={{0,2},{1,3},{2,4},{3,5},{4,6},{5,7},{6,8},{7,9},{8,10},{9,11},{10,... | collective-permute-start | bytes 1544 | tf_op jit(solution)/shard_map/ppermute | solution.py:20
  20.2 174.1 %collective-permute-start.5 = (bf16[128,512]{0,1:T(8,128)(2,1)S(1)}, bf16[128,512]{0,1:T(8,128)(2,1)}, u32[]{:S(2)}, u32[]{:S(2)}) collective-permute-start(bf16[128,512]{0,1:T(8,128)(2,1)S(1)} %copy.92), channel_id=1, source_target_pairs={{0,1},{1,2},{2,3},{3,4},{4,5},{5,6},{6,7},{7,8},{8,9},{9,10},{10,1... | collective-permute-start | bytes 393224 | tf_op jit(solution)/shard_map/ppermute | solution.py:20
  22.2 172.1 %collective-permute-start.4 = (bf16[128,512]{0,1:T(8,128)(2,1)S(1)}, bf16[128,512]{0,1:T(8,128)(2,1)}, u32[]{:S(2)}, u32[]{:S(2)}) collective-permute-start(bf16[128,512]{0,1:T(8,128)(2,1)S(1)} %copy.92), channel_id=1, source_target_pairs={{0,2},{1,3},{2,4},{3,5},{4,6},{5,7},{6,8},{7,9},{8,10},{9,11},{10,... | collective-permute-start | bytes 393224 | tf_op jit(solution)/shard_map/ppermute | solution.py:20
  25.5 167.6 %collective-permute-start = (bf16[128,512]{1,0:T(8,128)(2,1)}, bf16[128,512]{1,0:T(8,128)(2,1)}, u32[]{:S(2)}, u32[]{:S(2)}) collective-permute-start(bf16[128,512]{1,0:T(8,128)(2,1)} %param.14), channel_id=1, source_target_pairs={{0,2},{1,3},{2,4},{3,5},{4,6},{5,7},{6,8},{7,9},{8,10},{9,11},{10,... | collective-permute-start | bytes 393224 | tf_op jit(solution)/shard_map/ppermute | solution.py:20
  31.0 6.6 %copy-start.17 = (bf16[1024,256]{0,1:T(8,128)(2,1)S(1)}, bf16[1024,256]{0,1:T(8,128)(2,1)}, u32[]{:S(2)}) copy-start(bf16[1024,256]{0,1:T(8,128)(2,1)} %copy-done.16) | copy-start | bytes 1572868
  31.5 11.8 %copy-start.13 = (pred[512,1024]{1,0:T(8,128)(4,1)}, pred[512,1024]{1,0:T(8,128)(4,1)S(1)}, u32[]{:S(2)}) copy-start(pred[512,1024]{1,0:T(8,128)(4,1)S(1)} %iota_compare_fusion.1) | copy-start | bytes 1572868
  37.5 5.7 %copy-start.7 = (pred[512,1024]{1,0:T(8,128)(4,1)}, pred[512,1024]{1,0:T(8,128)(4,1)S(1)}, u32[]{:S(2)}) copy-start(pred[512,1024]{1,0:T(8,128)(4,1)S(1)} %get-tuple-element.36) | copy-start | bytes 1572868
  37.5 5.7 %copy-start.8 = (pred[512,1024]{1,0:T(8,128)(4,1)}, pred[512,1024]{1,0:T(8,128)(4,1)S(1)}, u32[]{:S(2)}) copy-start(pred[512,1024]{1,0:T(8,128)(4,1)S(1)} %get-tuple-element.37) | copy-start | bytes 1572868
  37.5 5.7 %copy-start.9 = (pred[512,1024]{1,0:T(8,128)(4,1)}, pred[512,1024]{1,0:T(8,128)(4,1)S(1)}, u32[]{:S(2)}) copy-start(pred[512,1024]{1,0:T(8,128)(4,1)S(1)} %get-tuple-element.38) | copy-start | bytes 1572868
  37.5 5.7 %copy-start.10 = (pred[512,1024]{1,0:T(8,128)(4,1)}, pred[512,1024]{1,0:T(8,128)(4,1)S(1)}, u32[]{:S(2)}) copy-start(pred[512,1024]{1,0:T(8,128)(4,1)S(1)} %get-tuple-element.39) | copy-start | bytes 1572868
  37.6 5.7 %copy-start.11 = (pred[512,1024]{1,0:T(8,128)(4,1)}, pred[512,1024]{1,0:T(8,128)(4,1)S(1)}, u32[]{:S(2)}) copy-start(pred[512,1024]{1,0:T(8,128)(4,1)S(1)} %get-tuple-element.40) | copy-start | bytes 1572868
  37.6 79.6 %copy-start.1 = (pred[512,1024]{1,0:T(8,128)(4,1)}, pred[512,1024]{1,0:T(8,128)(4,1)S(1)}, u32[]{:S(2)}) copy-start(pred[512,1024]{1,0:T(8,128)(4,1)S(1)} %get-tuple-element.47) | copy-start | bytes 1572868
  37.6 79.6 %copy-start.3 = (pred[512,1024]{1,0:T(8,128)(4,1)}, pred[512,1024]{1,0:T(8,128)(4,1)S(1)}, u32[]{:S(2)}) copy-start(pred[512,1024]{1,0:T(8,128)(4,1)S(1)} %get-tuple-element.48) | copy-start | bytes 1572868
  113.6 0.6 copy-start.23
  113.7 0.6 copy-start.24
  117.2 7.1 %copy-start.14 = (pred[512,1024]{1,0:T(8,128)(4,1)}, pred[512,1024]{1,0:T(8,128)(4,1)S(1)}, u32[]{:S(2)}) copy-start(pred[512,1024]{1,0:T(8,128)(4,1)S(1)} %iota_compare_fusion) | copy-start | bytes 1572868
  126.0 67.2 %collective-permute-start.1 = (bf16[128,512]{1,0:T(8,128)(2,1)}, bf16[128,512]{1,0:T(8,128)(2,1)S(1)}, u32[]{:S(2)}, u32[]{:S(2)}) collective-permute-start(bf16[128,512]{1,0:T(8,128)(2,1)} %param.14), channel_id=1, source_target_pairs={{0,1},{1,2},{2,3},{3,4},{4,5},{5,6},{6,7},{7,8},{8,9},{9,10},{10,1... | collective-permute-start | bytes 393224 | tf_op jit(solution)/shard_map/ppermute | solution.py:20
  158.8 8.5 %copy-start.19 = (f32[2,512,1]{1,0,2:T(2,128)S(1)}, f32[2,512,1]{1,0,2:T(2,128)}, u32[]{:S(2)}) copy-start(f32[2,512,1]{1,0,2:T(2,128)} %copy.186) | copy-start | bytes 12292
  158.8 8.5 %copy-start.20 = (f32[2,512,1]{1,0,2:T(2,128)S(1)}, f32[2,512,1]{1,0,2:T(2,128)}, u32[]{:S(2)}) copy-start(f32[2,512,1]{1,0,2:T(2,128)} %copy.187) | copy-start | bytes 12292
  158.8 8.5 %copy-start.21 = (f32[2,512,1]{1,0,2:T(2,128)S(1)}, f32[2,512,1]{1,0,2:T(2,128)}, u32[]{:S(2)}) copy-start(f32[2,512,1]{1,0,2:T(2,128)} %copy.188) | copy-start | bytes 12292
  158.8 8.5 %copy-start.22 = (f32[2,512,1]{1,0,2:T(2,128)S(1)}, f32[2,512,1]{1,0,2:T(2,128)}, u32[]{:S(2)}) copy-start(f32[2,512,1]{1,0,2:T(2,128)} %copy.189) | copy-start | bytes 12292
  167.3 6.6 %copy-start.2 = (pred[512,1024]{1,0:T(8,128)(4,1)S(1)}, pred[512,1024]{1,0:T(8,128)(4,1)}, u32[]{:S(2)}) copy-start(pred[512,1024]{1,0:T(8,128)(4,1)} %copy-done.1) | copy-start | bytes 1572868
  167.3 6.6 %copy-start.4 = (pred[512,1024]{1,0:T(8,128)(4,1)S(1)}, pred[512,1024]{1,0:T(8,128)(4,1)}, u32[]{:S(2)}) copy-start(pred[512,1024]{1,0:T(8,128)(4,1)} %copy-done.3) | copy-start | bytes 1572868
  167.3 6.6 %copy-start.5 = (pred[512,1024]{1,0:T(8,128)(4,1)S(1)}, pred[512,1024]{1,0:T(8,128)(4,1)}, u32[]{:S(2)}) copy-start(pred[512,1024]{1,0:T(8,128)(4,1)} %get-tuple-element.49) | copy-start | bytes 1572868
  167.3 6.6 %copy-start.6 = (pred[512,1024]{1,0:T(8,128)(4,1)S(1)}, pred[512,1024]{1,0:T(8,128)(4,1)}, u32[]{:S(2)}) copy-start(pred[512,1024]{1,0:T(8,128)(4,1)} %get-tuple-element.50) | copy-start | bytes 1572868
  167.3 6.6 %copy-start.15 = (pred[512,1024]{1,0:T(8,128)(4,1)S(1)}, pred[512,1024]{1,0:T(8,128)(4,1)}, u32[]{:S(2)}) copy-start(pred[512,1024]{1,0:T(8,128)(4,1)} %copy-done.14) | copy-start | bytes 1572868
  167.4 6.6 %copy-start.29 = (f32[2,512,1024]{2,1,0:T(8,128)S(1)}, f32[2,512,1024]{2,1,0:T(8,128)}, u32[]{:S(2)}) copy-start(f32[2,512,1024]{2,1,0:T(8,128)} %get-tuple-element.55) | copy-start | bytes 12582916
  173.9 18.9 %copy-start.25 = (s32[128]{0:T(128)S(1)}, s32[128]{0:T(128)}, u32[]{:S(2)}) copy-start(s32[128]{0:T(128)} %param.15) | copy-start | bytes 1540
  173.9 18.9 %copy-start.26 = (pred[384]{0:T(512)(128)(4,1)S(1)}, pred[384]{0:T(512)(128)(4,1)}, u32[]{:S(2)}) copy-start(pred[384]{0:T(512)(128)(4,1)} %broadcast_compare_fusion.10) | copy-start | bytes 1156
  174.0 18.9 %copy-start.27 = (s32[128]{0:T(128)S(1)}, s32[128]{0:T(128)}, u32[]{:S(2)}) copy-start(s32[128]{0:T(128)} %get-tuple-element.61) | copy-start | bytes 1540
  174.0 18.9 %copy-start.28 = (s32[128]{0:T(128)S(1)}, s32[128]{0:T(128)}, u32[]{:S(2)}) copy-start(s32[128]{0:T(128)} %get-tuple-element.62) | copy-start | bytes 1540
  174.0 19.2 %copy-start.18 = (bf16[128,512]{1,0:T(8,128)(2,1)S(1)}, bf16[128,512]{1,0:T(8,128)(2,1)}, u32[]{:S(2)}) copy-start(bf16[128,512]{1,0:T(8,128)(2,1)} %param.14) | copy-start | bytes 393220
  179.2 23.1 %all-to-all-start = ((bf16[8,128,256]{1,2,0:T(8,128)(2,1)}), bf16[8,128,256]{1,2,0:T(8,128)(2,1)S(1)}, u32[]{:S(2)}, u32[]{:S(2)}) async-start(bf16[8,128,256]{1,2,0:T(8,128)(2,1)} %copy_bitcast_fusion), calls=%async_computation | async-start | bytes 1048576 | tf_op jit(solution)/shard_map/all_to_all | solution.py:123
Sparse Core Ops, SparseCore 0:
  11.0 143.2 all-gather.2
where the time goes:
time: 216 us
  blocking collectives  70.3 us (33%)
  starting transfers between devices  42.6 us (20%)
  matrix products  41 us (19%)
  waiting for transfers between devices  21.4 us (10%)
  between operations  14.9 us (7%)
  local copies, waits for them, and re-layouts  13 us (6%)
  other arithmetic  12.5 us (6%)
    all_gather x1, blocking collectives, local(): lax.all_gather(own_sum[None].astype(jnp.bfloat16), 'ctx', axis=0, tiled=T...  70.3 us
    ppermute x6, starting transfers between devices, from_behind(): return lax.ppermute(value, axis, pairs)  29 us
    all_gather x1, waiting for transfers between devices, local(): lax.all_gather(own_state[None].astype(jnp.bfloat16), 'ctx', axis=0, tiled...  15.4 us
    all_to_all x1, starting transfers between devices, local(): lax.all_to_all(queries_gated, 'head', split_axis=0, concat_axis=1, tiled=...  13.6 us
    dot_general x2, matrix products, local(): jnp.einsum('tha,sha->hts', q_blk, k_feats, preferred_element_type=jnp.flo...  12.7 us
    dot_general x2, matrix products, local(): jnp.einsum('hts,shb->thb', weight, v_heads, preferred_element_type=jnp.fl...  10.6 us
    unnamed x78, local copies, waits for them, and re-layouts  8.9 us
    all_to_all x1, waiting for transfers between devices, local(): lax.all_to_all(queries_gated, 'head', split_axis=0, concat_axis=1, tiled=...  5.92 us
  transfers between devices with their start and end apart: 8, of which 2 were waited for; matrix products, arithmetic and copies ran while one was open for 26% of the time, Pallas kernels for 0%

commit v1 on v0

v1 whole, which is shorter than its diff:
```python
import functools

import jax
import jax.numpy as jnp
from jax import lax
from jax.experimental import pallas as pl
from jax.experimental.pallas import tpu as pltpu
from jax.sharding import Mesh
from jax.sharding import PartitionSpec as P

H = 16
E = 128
KVH = 4
NCLASS = 16
HEADS = 2
TOK = 1024
TILE = 128
SUMS = HEADS * E
ROWS = SUMS + 16
F32 = jnp.float32
BF16 = jnp.bfloat16
LOG2E = 1.4426950408889634


def feats(x):
    x = x.astype(F32)
    return jnp.where(x > 0, x + 1.0, jnp.exp(x)).astype(BF16)


def dot_nn(a, b):
    return lax.dot_general(a, b, (((1,), (0,)), ((), ())), preferred_element_type=F32)


def dot_nt(a, b):
    return lax.dot_general(a, b, (((1,), (1,)), ((), ())), preferred_element_type=F32)


def dot_tn(a, b):
    return lax.dot_general(a, b, (((0,), (0,)), ((), ())), preferred_element_type=F32)


def hi_lo(x):
    hi = x.astype(BF16)
    return hi, (x - hi.astype(F32)).astype(BF16)


def head_cols(h):
    return slice(h * E, (h + 1) * E)


def sum_rows(sums):
    row = lax.broadcasted_iota(jnp.int32, (16, E), 0)
    out = jnp.zeros((16, E), F32)
    for h in range(HEADS):
        hi = sums[h].astype(BF16).astype(F32)
        out = jnp.where(row == h, hi, out)
        out = jnp.where(row == HEADS + h, sums[h] - hi, out)
    return out.astype(BF16)


def state_kernel(k_ref, v_ref, s_ref):
    sums = []
    for h in range(HEADS):
        kf = feats(k_ref[:, head_cols(h)])
        state = dot_tn(kf, v_ref[:, head_cols(h)]).astype(BF16)
        sums.append(dot_nn(jnp.ones((8, TOK), BF16), kf)[0:1])
        for copy in range(4):
            s_ref[copy, head_cols(h), :] = state
    rows = sum_rows(sums)
    for copy in range(4):
        s_ref[copy, SUMS:ROWS, :] = rows


def total_kernel(r_ref, s_ref):
    total = r_ref[0].astype(F32)
    for j in range(1, 4):
        total = total + r_ref[j].astype(F32)
    state = total[:SUMS].astype(BF16)
    tail = total[SUMS:]
    rows = sum_rows([tail[h : h + 1] + tail[HEADS + h : HEADS + h + 1] for h in range(HEADS)])
    for copy in range(4):
        s_ref[copy, :SUMS, :] = state
        s_ref[copy, SUMS:ROWS, :] = rows


def table_parts(tab):
    hi = tab.astype(BF16)
    rest = tab - hi.astype(F32)
    mid = rest.astype(BF16)
    low = (rest - mid.astype(F32)).astype(BF16)
    return jnp.concatenate([hi, mid, low], axis=0)


def tile_weights(cls_row, tab3):
    hot = lax.broadcasted_iota(jnp.int32, (NCLASS, TILE), 0) == cls_row
    hot = jnp.where(hot, 1.0, 0.0).astype(BF16)
    return dot_tn(jnp.concatenate([hot, hot, hot], axis=0), tab3)


def local_kernel(q_ref, k_ref, v_ref, cls_ref, tab_ref, part_ref):
    t_row = lax.broadcasted_iota(jnp.int32, (TILE, TILE), 0)
    s_col = lax.broadcasted_iota(jnp.int32, (TILE, TILE), 1)
    same = (t_row // 64) == (s_col // 64)
    mask0 = same & (s_col <= t_row)
    mask1 = (t_row >= 64) & (s_col < 64)
    lane = s_col
    row_id = t_row
    tiles = TOK // TILE
    for h in range(HEADS):
        cols = head_cols(h)
        tab3 = table_parts(tab_ref[h])
        kf = [feats(k_ref[i * TILE : (i + 1) * TILE, cols]) for i in range(tiles)]
        vt = [v_ref[i * TILE : (i + 1) * TILE, cols] for i in range(tiles)]
        state = [dot_tn(kf[i], vt[i]) for i in range(tiles - 1)]
        ksum = [jnp.sum(kf[i].astype(F32), axis=0, keepdims=True) for i in range(tiles - 1)]
        group = {}
        for level, size in ((2, 1), (3, 2), (4, 4)):
            for first in range(0, tiles, 2 * size):
                st = state[first]
                ks = ksum[first]
                for other in range(first + 1, first + size):
                    st = st + state[other]
                    ks = ks + ksum[other]
                group[level, first] = (jnp.concatenate(hi_lo(st), axis=0), ks)
        for i in range(tiles):
            rows = slice(i * TILE, (i + 1) * TILE)
            qf = feats(q_ref[rows, cols])
            qq = jnp.concatenate([qf, qf], axis=1)
            sc = dot_nt(qf, kf[i])
            s0 = jnp.where(mask0, sc, 0.0)
            s1 = jnp.where(mask1, sc, 0.0)
            den = jnp.where(lane == 0, jnp.sum(s0, axis=1, keepdims=True), 0.0)
            den = jnp.where(lane == 1, jnp.sum(s1, axis=1, keepdims=True), den)
            far = []
            for level, size in ((2, 1), (3, 2), (4, 4)):
                if i & size:
                    far.append((level, group[level, i // (2 * size) * 2 * size]))
            if far:
                ks = jnp.zeros((TILE, E), F32)
                for level, (_, row) in far:
                    ks = jnp.where(row_id == level, row, ks)
                den = den + dot_nt(qq, jnp.concatenate(hi_lo(ks), axis=1))
            coeff = tile_weights(cls_ref[i : i + 1, :], tab3) / jnp.maximum(den, 1.0)
            weight = coeff[:, 0:1] * s0 + coeff[:, 1:2] * s1
            acc = dot_nn(weight.astype(BF16), vt[i])
            for level, (st, _) in far:
                acc = acc + coeff[:, level : level + 1] * dot_nn(qq, st)
            part_ref[rows, cols] = acc


def two_levels(axis, first_lane, r_ref, q_ref, cls_ref, tab_ref, part_ref, emit):
    me = lax.axis_index(axis)
    bit0 = (me & 1).astype(F32)
    bit1 = (me >> 1).astype(F32)
    near = r_ref[jnp.maximum(me - 1, 0)].astype(F32) * bit0
    wide = (r_ref[0].astype(F32) + r_ref[1].astype(F32)) * bit1
    row_id = lax.broadcasted_iota(jnp.int32, (TILE, E), 0)
    for h in range(HEADS):
        cols = head_cols(h)
        tab3 = table_parts(tab_ref[h])
        near_hi, near_lo = hi_lo(near[cols])
        wide_hi, wide_lo = hi_lo(wide[cols])
        state = jnp.concatenate(
            [
                jnp.concatenate([near_hi, wide_hi], axis=1),
                jnp.concatenate([near_lo, wide_lo], axis=1),
            ],
            axis=0,
        )
        a, b = SUMS + h, SUMS + HEADS + h
        ks = jnp.where(row_id == first_lane, near[a : a + 1] + near[b : b + 1], 0.0)
        ks = jnp.where(row_id == first_lane + 1, wide[a : a + 1] + wide[b : b + 1], ks)
        ks = jnp.concatenate(hi_lo(ks), axis=1)
        for i in range(TOK // TILE):
            rows = slice(i * TILE, (i + 1) * TILE)
            qf = feats(q_ref[rows, cols])
            qq = jnp.concatenate([qf, qf], axis=1)
            den = dot_nt(qq, ks)
            through = dot_nn(qq, state)
            coeff = tile_weights(cls_ref[i : i + 1, :], tab3) / jnp.maximum(den, 1.0)
            acc = part_ref[rows, cols]
            acc = acc + coeff[:, first_lane : first_lane + 1] * through[:, :E]
            acc = acc + coeff[:, first_lane + 1 : first_lane + 2] * through[:, E:]
            emit(rows, cols, acc)


def level_kernel(axis, first_lane, r_ref, q_ref, cls_ref, tab_ref, part_ref, out_ref):
    def emit(rows, cols, acc):
        out_ref[rows, cols] = acc

    two_levels(axis, first_lane, r_ref, q_ref, cls_ref, tab_ref, part_ref, emit)


def final_kernel(axis, first_lane, r_ref, q_ref, cls_ref, tab_ref, part_ref, mixed_ref, gated_ref):
    def emit(rows, cols, acc):
        mixed = acc.astype(BF16)
        mixed_ref[rows, cols] = mixed
        gate = 0.5 + 1.0 / (1.0 + jnp.exp(-mixed.astype(F32)))
        gated_ref[rows.start // TILE, :, cols] = (q_ref[rows, cols].astype(F32) * gate).astype(BF16)

    two_levels(axis, first_lane, r_ref, q_ref, cls_ref, tab_ref, part_ref, emit)


def window_kernel(xq_ref, k_ref, v_ref, seg_ref, rim1_ref, rim2_ref, out_ref):
    place = (
        (lax.axis_index("x") * 4 + lax.axis_index("zh")) * 4 + lax.axis_index("zl")
    ) * 8 + lax.axis_index("head")
    seg_own = seg_ref[0:1, :].astype(F32)
    seg_q = jnp.transpose(jnp.broadcast_to(seg_own, (TILE, TILE)))
    t_row = lax.broadcasted_iota(jnp.int32, (TILE, TILE), 0)
    s_col = lax.broadcasted_iota(jnp.int32, (TILE, TILE), 1)
    low = -1e30
    seg2 = rim2_ref[TILE : TILE + 1, :TILE].astype(F32)
    seg1 = rim1_ref[TILE : TILE + 1, :TILE].astype(F32)
    bias2 = jnp.where((seg_q == seg2) & (s_col > t_row) & (place >= 2), 0.0, low)
    bias1 = jnp.where((seg_q == seg1) & (place >= 1), 0.0, low)
    bias0 = jnp.where((seg_q == seg_own) & (s_col <= t_row), 0.0, low)
    bias = jnp.concatenate([bias2, bias1, bias0], axis=1)
    scale = E ** (-0.5) * LOG2E
    ones = jnp.ones((3 * TILE, E), BF16)
    for g in range(KVH):
        cols = slice(g * E, (g + 1) * E)
        vcols = slice((KVH + g) * E, (KVH + g + 1) * E)
        keys = jnp.concatenate([rim2_ref[:TILE, cols], rim1_ref[:TILE, cols], k_ref[:, cols]], axis=0)
        vals = jnp.concatenate([rim2_ref[:TILE, vcols], rim1_ref[:TILE, vcols], v_ref[:, cols]], axis=0)
        vals = jnp.concatenate([vals, ones], axis=1)
        for j in range(H // KVH):
            src, part = 2 * g + j // 2, j % 2
            sc = dot_nt(xq_ref[src, :, head_cols(part)], keys) * scale + bias
            top = jnp.max(sc, axis=1, keepdims=True)
            probs = jnp.exp2(sc - top).astype(BF16)
            res = dot_nn(probs, vals)
            head = g * (H // KVH) + j
            out_ref[:, head_cols(head)] = (res[:, :E] / res[:, E:]).astype(BF16)


def call(kernel, out, *args, aliases=None):
    return pl.pallas_call(
        kernel,
        out_shape=out,
        input_output_aliases=aliases or {},
        compiler_params=pltpu.CompilerParams(vmem_limit_bytes=40 * 1024 * 1024),
    )(*args)


def swap(value, axis):
    return lax.all_to_all(value, axis, split_axis=0, concat_axis=0, tiled=True)


def local(queries, lin_keys, lin_values, level_class, level_table, win_keys, win_values, seg_ids):
    sds = jax.ShapeDtypeStruct
    levels = level_table.shape[2]
    copies = sds((4, ROWS, E), BF16)
    part_shape = sds((TOK, HEADS * E), F32)
    own = call(state_kernel, copies, lin_keys, lin_values)
    from_zl = swap(own, "zl")
    cls = level_class.reshape(TOK // TILE, TILE)
    tab = jnp.pad(jnp.transpose(level_table, (1, 0, 2)), ((0, 0), (0, 0), (0, E - levels)))
    part = call(local_kernel, part_shape, queries, lin_keys, lin_values, cls, tab)
    from_zh = swap(call(total_kernel, copies, from_zl), "zh")
    seg_row = jnp.pad(seg_ids.astype(BF16)[None], ((0, 15), (0, 2 * KVH * E - TILE)))
    packed = jnp.concatenate([jnp.concatenate([win_keys, win_values], axis=1), seg_row], axis=0)
    flat = ("x", "zh", "zl", "head")
    rims = [lax.ppermute(packed, flat, [(i, i + d) for i in range(512 - d)]) for d in (1, 2)]
    part = call(
        functools.partial(level_kernel, "zl", 5), part_shape, from_zl, queries, cls, tab, part, aliases={4: 0}
    )
    from_x = swap(call(total_kernel, copies, from_zh), "x")
    part = call(
        functools.partial(level_kernel, "zh", 7), part_shape, from_zh, queries, cls, tab, part, aliases={4: 0}
    )
    mixed, gated = call(
        functools.partial(final_kernel, "x", 9),
        (sds((TOK, HEADS * E), BF16), sds((8, TILE, HEADS * E), BF16)),
        from_x,
        queries,
        cls,
        tab,
        part,
    )
    token_q = swap(gated, "head")
    out = call(
        window_kernel,
        sds((TILE, H * E), BF16),
        token_q,
        win_keys,
        win_values,
        jnp.broadcast_to(seg_ids[None], (8, TILE)),
        rims[0],
        rims[1],
    )
    return mixed, out


def solution(mesh):
    grid = Mesh(mesh.devices.reshape(4, 4, 4, 8), ("x", "zh", "zl", "head"))
    ctx = ("x", "zh", "zl")
    both = ("x", "zh", "zl", "head")
    return jax.shard_map(
        local,
        mesh=grid,
        in_specs=(
            P(ctx, "head"),
            P(ctx, "head"),
            P(ctx, "head"),
            P(ctx),
            P(None, "head", None),
            P(both, None),
            P(both, None),
            P(both),
        ),
        out_specs=(P(ctx, "head"), P(both, None)),
        check_vma=False,
    )
```

time: 216 us -> 94.1 us (0.44)
  the two profiles are of different devices: /device:TPU:1 before, /device:TPU:3 now
where the time goes in v1:
time: 94.1 us; the launch traced here: 93.6 us
  blocking collectives  41.3 us (44%)
  starting transfers between devices  22.2 us (24%)
  Pallas kernels  14.1 us (15%)
  waiting for transfers between devices  12.4 us (13%)
  local copies, waits for them, and re-layouts  2.77 us (3%)
    all_to_all x2, blocking collectives, swap(): return lax.all_to_all(value, axis, split_axis=0, concat_axis=0, tiled=True)  41.3 us
    all_to_all x2, starting transfers between devices, swap(): return lax.all_to_all(value, axis, split_axis=0, concat_axis=0, tiled=True)  15.5 us
    pallas_call x8, Pallas kernels, call(): pl.pallas_call(kernel, out_shape=out, input_output_aliases=aliases or {},...  14.1 us
    ppermute x2, waiting for transfers between devices, local(): lax.ppermute(packed, flat, [(i, i + d) for i in range(512 - d)])  12.4 us
    ppermute x2, starting transfers between devices, local(): lax.ppermute(packed, flat, [(i, i + d) for i in range(512 - d)])  6.63 us
    unnamed x21, local copies, waits for them, and re-layouts  2.77 us
  transfers between devices with their start and end apart: 4, of which 2 were waited for; matrix products, arithmetic and copies ran while one was open for 0% of the time, Pallas kernels for 9%

profile of v1, /device:TPU:3, one launch (start us, length us, event | category | flops | bytes accessed | tf_op | source)
XLA Modules:
  0.0 93.6 jit_solution(731268938111578446)
XLA Ops:
  0.6 0.0 copy-start.1
  0.6 1.0 %copy-done.1 = bf16[1024,256]{1,0:T(8,128)(2,1)S(1)} copy-done((bf16[1024,256]{1,0:T(8,128)(2,1)S(1)}, bf16[1024,256]{1,0:T(8,128)(2,1)}, u32[]{:S(2)}) %copy-start.1) | copy-done | bytes 524312
  1.7 0.0 copy-start.3
  1.7 1.0 %copy-done.3 = bf16[1024,256]{1,0:T(8,128)(2,1)S(1)} copy-done((bf16[1024,256]{1,0:T(8,128)(2,1)S(1)}, bf16[1024,256]{1,0:T(8,128)(2,1)}, u32[]{:S(2)}) %copy-start.3) | copy-done | bytes 524312
  2.7 0.4 shard_map.95
  3.2 12.8 %all_to_all.20.r_ref = bf16[4,272,128]{2,1,0:T(8,128)(2,1)S(1)} all-to-all(bf16[4,272,128]{2,1,0:T(8,128)(2,1)S(1)} %shard_map.95), channel_id=1, replica_groups=mesh['x'=4,'zh'=4,'zl'=4,'head'=8] {'zl'}, dimensions={0} | all-to-all | bytes 557056 | tf_op jit(solution)/shard_map/all_to_all | solution.py:247
  16.0 0.0 copy-start.4
  16.0 28.5 %all_to_all.21.r_ref = bf16[4,272,128]{2,1,0:T(8,128)(2,1)S(1)} all-to-all(bf16[4,272,128]{2,1,0:T(8,128)(2,1)S(1)} %shard_map.96), channel_id=1, replica_groups=mesh['x'=4,'zh'=4,'zl'=4,'head'=8] {'zh'}, dimensions={0} | all-to-all | bytes 557056 | tf_op jit(solution)/shard_map/all_to_all | solution.py:247
  44.5 0.0 copy-start
  44.5 0.0 copy-start.2
  44.5 0.8 shard_map.97
  45.3 0.0 copy-start.8
  45.3 4.4 %all-to-all-start.2 = ((bf16[4,272,128]{2,1,0:T(8,128)(2,1)}), bf16[4,272,128]{2,1,0:T(8,128)(2,1)S(1)}, u32[]{:S(2)}, u32[]{:S(2)}) async-start(bf16[4,272,128]{2,1,0:T(8,128)(2,1)} %shard_map.97), calls=%async_computation.2 | async-start | bytes 557056 | tf_op jit(solution)/shard_map/all_to_all | solution.py:247
  49.7 0.0 copy-done.8
  49.7 0.0 copy-start.7
  49.7 0.1 copy.12
  49.8 0.0 copy-done.4
  49.8 0.0 copy-done
  49.8 0.0 copy-done.2
  49.8 0.6 copy-done.7
  50.4 5.3 %shard_map.98.part_ref = f32[1024,256]{1,0:T(8,128)S(1)} custom-call(bf16[1024,256]{1,0:T(8,128)(2,1)S(1)} %copy-done, bf16[1024,256]{1,0:T(8,128)(2,1)S(1)} %copy-done.2, bf16[1024,256]{1,0:T(8,128)(2,1)S(1)} %copy-done.4, s32[8,128]{1,0:T(8,128)S(1)} %bitcast.4, f32[2,16,128]{2,1,0:T(8,128)S(1)} %pad.8.tab_ref), custom_call_target="tpu_custom_call" | custom-call | tf_op jit(solution)/shard_map/pallas_call | solution.py:238
  55.6 1.5 %shard_map.99.part_ref = f32[1024,256]{1,0:T(8,128)S(1)} custom-call(bf16[4,272,128]{2,1,0:T(8,128)(2,1)S(1)} %all_to_all.20.r_ref, bf16[1024,256]{1,0:T(8,128)(2,1)S(1)} %copy-done, s32[8,128]{1,0:T(8,128)S(1)} %bitcast.5, f32[2,16,128]{2,1,0:T(8,128)S(1)} %pad.8.tab_ref, f32[1024,256]{1,0:T(8,128)S(1)} %shard_map.98.part_ref), custom_call_target="tpu_custom_call", output_to_operand_aliasing={{}: (4, {})} | custom-call | tf_op jit(solution)/shard_map/pallas_call | solution.py:238
  57.1 1.5 %shard_map.100.part_ref = f32[1024,256]{1,0:T(8,128)S(1)} custom-call(bf16[4,272,128]{2,1,0:T(8,128)(2,1)S(1)} %all_to_all.21.r_ref, bf16[1024,256]{1,0:T(8,128)(2,1)S(1)} %copy-done, s32[8,128]{1,0:T(8,128)S(1)} %bitcast.6, f32[2,16,128]{2,1,0:T(8,128)S(1)} %pad.8.tab_ref, f32[1024,256]{1,0:T(8,128)S(1)} %shard_map.99.part_ref), custom_call_target="tpu_custom_call", output_to_operand_aliasing={{}: (4, {})} | custom-call | tf_op jit(solution)/shard_map/pallas_call | solution.py:238
  58.6 0.0 all-to-all-done.2.r_ref
  58.6 2.3 %shard_map.101 = (bf16[1024,256]{1,0:T(8,128)(2,1)}, bf16[8,128,256]{2,1,0:T(8,128)(2,1)}) custom-call(bf16[4,272,128]{2,1,0:T(8,128)(2,1)S(1)} %all-to-all-done.2.r_ref, bf16[1024,256]{1,0:T(8,128)(2,1)S(1)} %copy-done, s32[8,128]{1,0:T(8,128)S(1)} %bitcast.7, f32[2,16,128]{2,1,0:T(8,128)S(1)} %pad.8.tab_ref, f32[1024,256]{1,0:T(8,128)S(1)} %shard_map.100.part_ref), custom_call_target="tpu_custom_call" | custom-call | tf_op jit(solution)/shard_map/pallas_call | solution.py:238
  60.9 0.0 copy-start.9
  60.9 0.0 copy-start.5
  60.9 0.0 copy-start.6
  60.9 11.1 %all-to-all-start.3 = ((bf16[8,128,256]{2,1,0:T(8,128)(2,1)}), bf16[8,128,256]{2,1,0:T(8,128)(2,1)S(1)}, u32[]{:S(2)}, u32[]{:S(2)}) async-start(bf16[8,128,256]{2,1,0:T(8,128)(2,1)} %get-tuple-element.5), calls=%async_computation.3 | async-start | bytes 1048576 | tf_op jit(solution)/shard_map/all_to_all | solution.py:247
  72.0 0.0 copy-done.9
  72.0 0.0 copy-done.5
  72.1 0.0 copy-done.6
  72.1 3.5 %collective-permute-start = (bf16[144,1024]{1,0:T(8,128)(2,1)S(1)}, bf16[144,1024]{1,0:T(8,128)(2,1)S(1)}, u32[]{:S(2)}, u32[]{:S(2)}) collective-permute-start(bf16[144,1024]{1,0:T(8,128)(2,1)S(1)} %fusion.1), channel_id=1, source_target_pairs={{0,1},{1,2},{2,3},{3,4},{4,5},{5,6},{6,7},{7,8},{8,9},{9,10},{10,1... | collective-permute-start | bytes 884744 | tf_op jit(solution)/shard_map/ppermute | solution.py:264
  75.6 3.1 %collective-permute-start.1 = (bf16[144,1024]{1,0:T(8,128)(2,1)S(1)}, bf16[144,1024]{1,0:T(8,128)(2,1)S(1)}, u32[]{:S(2)}, u32[]{:S(2)}) collective-permute-start(bf16[144,1024]{1,0:T(8,128)(2,1)S(1)} %fusion.1), channel_id=1, source_target_pairs={{0,2},{1,3},{2,4},{3,5},{4,6},{5,7},{6,8},{7,9},{8,10},{9,11},{10,... | collective-permute-start | bytes 884744 | tf_op jit(solution)/shard_map/ppermute | solution.py:264
  78.7 5.6 %collective-permute-done.rim1_ref = bf16[144,1024]{1,0:T(8,128)(2,1)S(1)} collective-permute-done((bf16[144,1024]{1,0:T(8,128)(2,1)S(1)}, bf16[144,1024]{1,0:T(8,128)(2,1)S(1)}, u32[]{:S(2)}, u32[]{:S(2)}) %collective-permute-start) | collective-permute-done | bytes 294944 | tf_op jit(solution)/shard_map/ppermute | solution.py:264
  84.3 6.9 %collective-permute-done.1.rim2_ref = bf16[144,1024]{1,0:T(8,128)(2,1)S(1)} collective-permute-done((bf16[144,1024]{1,0:T(8,128)(2,1)S(1)}, bf16[144,1024]{1,0:T(8,128)(2,1)S(1)}, u32[]{:S(2)}, u32[]{:S(2)}) %collective-permute-start.1) | collective-permute-done | bytes 294944 | tf_op jit(solution)/shard_map/ppermute | solution.py:264
  91.2 0.0 all-to-all-done.3.xq_ref
  91.2 2.4 %shard_map.102 = bf16[128,2048]{1,0:T(8,128)(2,1)} custom-call(bf16[8,128,256]{2,1,0:T(8,128)(2,1)S(1)} %all-to-all-done.3.xq_ref, bf16[128,512]{1,0:T(8,128)(2,1)S(1)} %copy-done.5, bf16[128,512]{1,0:T(8,128)(2,1)S(1)} %copy-done.6, s32[8,128]{1,0:T(8,128)S(1)} %broadcast_in_dim.4.seg_ref, bf16[144,1024]{1,0:T(8,128)(2,1)S(1)} %collective-permute-done.rim1_ref, ...), custom_call_target="tpu_custom_call" | custom-call | tf_op jit(solution)/shard_map/pallas_call | solution.py:238
  (5 shorter events, 0.1 us)
Async XLA Ops:
  0.6 1.0 %copy-start.1 = (bf16[1024,256]{1,0:T(8,128)(2,1)S(1)}, bf16[1024,256]{1,0:T(8,128)(2,1)}, u32[]{:S(2)}) copy-start(bf16[1024,256]{1,0:T(8,128)(2,1)} %k_ref.4) | copy-start | bytes 1572868
  1.7 1.0 %copy-start.3 = (bf16[1024,256]{1,0:T(8,128)(2,1)S(1)}, bf16[1024,256]{1,0:T(8,128)(2,1)}, u32[]{:S(2)}) copy-start(bf16[1024,256]{1,0:T(8,128)(2,1)} %v_ref.4) | copy-start | bytes 1572868
  16.0 33.8 %copy-start.4 = (bf16[1024,256]{1,0:T(8,128)(2,1)S(1)}, bf16[1024,256]{1,0:T(8,128)(2,1)}, u32[]{:S(2)}) copy-start(bf16[1024,256]{1,0:T(8,128)(2,1)} %v_ref.4) | copy-start | bytes 1572868
  44.5 5.3 %copy-start = (bf16[1024,256]{1,0:T(8,128)(2,1)S(1)}, bf16[1024,256]{1,0:T(8,128)(2,1)}, u32[]{:S(2)}) copy-start(bf16[1024,256]{1,0:T(8,128)(2,1)} %q_ref.7) | copy-start | bytes 1572868
  44.5 5.3 %copy-start.2 = (bf16[1024,256]{1,0:T(8,128)(2,1)S(1)}, bf16[1024,256]{1,0:T(8,128)(2,1)}, u32[]{:S(2)}) copy-start(bf16[1024,256]{1,0:T(8,128)(2,1)} %k_ref.4) | copy-start | bytes 1572868
  45.3 4.4 %copy-start.8 = (f32[16,2,11]{0,1,2:T(2,128)S(1)}, f32[16,2,11]{0,1,2:T(2,128)}, u32[]{:S(2)}) copy-start(f32[16,2,11]{0,1,2:T(2,128)} %param.12) | copy-start | bytes 4228
  45.3 13.4 %all-to-all-start.2 = ((bf16[4,272,128]{2,1,0:T(8,128)(2,1)}), bf16[4,272,128]{2,1,0:T(8,128)(2,1)S(1)}, u32[]{:S(2)}, u32[]{:S(2)}) async-start(bf16[4,272,128]{2,1,0:T(8,128)(2,1)} %shard_map.97), calls=%async_computation.2 | async-start | bytes 557056 | tf_op jit(solution)/shard_map/all_to_all | solution.py:247
  49.7 0.7 copy-start.7
  60.9 11.1 %copy-start.9 = (s32[128]{0:T(128)S(1)}, s32[128]{0:T(128)}, u32[]{:S(2)}) copy-start(s32[128]{0:T(128)} %param.15) | copy-start | bytes 1540
  60.9 11.2 %copy-start.5 = (bf16[128,512]{1,0:T(8,128)(2,1)S(1)}, bf16[128,512]{1,0:T(8,128)(2,1)}, u32[]{:S(2)}) copy-start(bf16[128,512]{1,0:T(8,128)(2,1)} %k_ref.5) | copy-start | bytes 393220
  60.9 11.2 %copy-start.6 = (bf16[128,512]{1,0:T(8,128)(2,1)S(1)}, bf16[128,512]{1,0:T(8,128)(2,1)}, u32[]{:S(2)}) copy-start(bf16[128,512]{1,0:T(8,128)(2,1)} %v_ref.5) | copy-start | bytes 393220
  60.9 30.3 %all-to-all-start.3 = ((bf16[8,128,256]{2,1,0:T(8,128)(2,1)}), bf16[8,128,256]{2,1,0:T(8,128)(2,1)S(1)}, u32[]{:S(2)}, u32[]{:S(2)}) async-start(bf16[8,128,256]{2,1,0:T(8,128)(2,1)} %get-tuple-element.5), calls=%async_computation.3 | async-start | bytes 1048576 | tf_op jit(solution)/shard_map/all_to_all | solution.py:247
  72.1 12.2 %collective-permute-start = (bf16[144,1024]{1,0:T(8,128)(2,1)S(1)}, bf16[144,1024]{1,0:T(8,128)(2,1)S(1)}, u32[]{:S(2)}, u32[]{:S(2)}) collective-permute-start(bf16[144,1024]{1,0:T(8,128)(2,1)S(1)} %fusion.1), channel_id=1, source_target_pairs={{0,1},{1,2},{2,3},{3,4},{4,5},{5,6},{6,7},{7,8},{8,9},{9,10},{10,1... | collective-permute-start | bytes 884744 | tf_op jit(solution)/shard_map/ppermute | solution.py:264
  75.6 15.5 %collective-permute-start.1 = (bf16[144,1024]{1,0:T(8,128)(2,1)S(1)}, bf16[144,1024]{1,0:T(8,128)(2,1)S(1)}, u32[]{:S(2)}, u32[]{:S(2)}) collective-permute-start(bf16[144,1024]{1,0:T(8,128)(2,1)S(1)} %fusion.1), channel_id=1, source_target_pairs={{0,2},{1,3},{2,4},{3,5},{4,6},{5,7},{6,8},{7,9},{8,10},{9,11},{10,... | collective-permute-start | bytes 884744 | tf_op jit(solution)/shard_map/ppermute | solution.py:264

commit v2 on v1

--- a/solution.py
+++ b/solution.py
@@ -15,6 +15,8 @@
 HEADS = 2
 TOK = 1024
 TILE = 128
+CHUNK = 256
+CHUNKS = TOK // CHUNK
 SUMS = HEADS * E
 ROWS = SUMS + 16
 F32 = jnp.float32
@@ -58,16 +60,31 @@
     return out.astype(BF16)
 
 
-def state_kernel(k_ref, v_ref, s_ref):
-    sums = []
-    for h in range(HEADS):
-        kf = feats(k_ref[:, head_cols(h)])
-        state = dot_tn(kf, v_ref[:, head_cols(h)]).astype(BF16)
-        sums.append(dot_nn(jnp.ones((8, TOK), BF16), kf)[0:1])
-        for copy in range(4):
-            s_ref[copy, head_cols(h), :] = state
-    rows = sum_rows(sums)
+def state_kernel(k_hbm, v_hbm, s_ref, k_ref, v_ref, sems):
+    copies = []
+    for i in range(CHUNKS):
+        rows = slice(i * CHUNK, (i + 1) * CHUNK)
+        pair = [
+            pltpu.make_async_copy(src.at[rows], dst.at[rows], sems.at[n, i])
+            for n, (src, dst) in enumerate(((k_hbm, k_ref), (v_hbm, v_ref)))
+        ]
+        for copy in pair:
+            copy.start()
+        copies.append(pair)
+    state = [jnp.zeros((E, E), F32) for _ in range(HEADS)]
+    sums = [jnp.zeros((8, E), F32) for _ in range(HEADS)]
+    for i in range(CHUNKS):
+        rows = slice(i * CHUNK, (i + 1) * CHUNK)
+        for copy in copies[i]:
+            copy.wait()
+        for h in range(HEADS):
+            kf = feats(k_ref[rows, head_cols(h)])
+            state[h] = state[h] + dot_tn(kf, v_ref[rows, head_cols(h)])
+            sums[h] = sums[h] + dot_nn(jnp.ones((8, CHUNK), BF16), kf)
+    rows = sum_rows([sums[h][0:1] for h in range(HEADS)])
     for copy in range(4):
+        for h in range(HEADS):
+            s_ref[copy, head_cols(h), :] = state[h].astype(BF16)
         s_ref[copy, SUMS:ROWS, :] = rows
 
 
@@ -234,13 +251,43 @@
             out_ref[:, head_cols(head)] = (res[:, :E] / res[:, E:]).astype(BF16)
 
 
-def call(kernel, out, *args, aliases=None):
+def call(kernel, out, *args, after=(), aliases=None):
+    count = len(args)
+
+    def body(*refs):
+        kernel(*refs[:count], *refs[count + len(after) :])
+
+    vmem = pl.BlockSpec(memory_space=pltpu.VMEM)
     return pl.pallas_call(
-        kernel,
+        body,
         out_shape=out,
+        in_specs=[vmem] * count + [pl.BlockSpec(memory_space=pl.ANY)] * len(after),
         input_output_aliases=aliases or {},
-        compiler_params=pltpu.CompilerParams(vmem_limit_bytes=40 * 1024 * 1024),
-    )(*args)
+        compiler_params=pltpu.CompilerParams(vmem_limit_bytes=32 * 1024 * 1024),
+    )(*args, *after)
+
+
+def span_state(keys, values):
+    hbm = pl.BlockSpec(memory_space=pltpu.HBM)
+    return pl.pallas_call(
+        state_kernel,
+        out_shape=jax.ShapeDtypeStruct((4, ROWS, E), BF16),
+        in_specs=[hbm, hbm],
+        scratch_shapes=[
+            pltpu.VMEM((TOK, HEADS * E), BF16),
+            pltpu.VMEM((TOK, HEADS * E), BF16),
+            pltpu.SemaphoreType.DMA((2, CHUNKS)),
+        ],
+        compiler_params=pltpu.CompilerParams(vmem_limit_bytes=60 * 1024 * 1024),
+    )(keys, values)
+
+
+def pack_kernel(k_ref, v_ref, seg_ref, out_ref):
+    width = KVH * E
+    out_ref[:TILE, :width] = k_ref[...]
+    out_ref[:TILE, width:] = v_ref[...]
+    out_ref[TILE:, :] = jnp.zeros((16, 2 * width), BF16)
+    out_ref[TILE:, :TILE] = jnp.broadcast_to(seg_ref[0:1, :].astype(F32), (16, TILE)).astype(BF16)
 
 
 def swap(value, axis):
@@ -252,22 +299,43 @@
     levels = level_table.shape[2]
     copies = sds((4, ROWS, E), BF16)
     part_shape = sds((TOK, HEADS * E), F32)
-    own = call(state_kernel, copies, lin_keys, lin_values)
-    from_zl = swap(own, "zl")
     cls = level_class.reshape(TOK // TILE, TILE)
     tab = jnp.pad(jnp.transpose(level_table, (1, 0, 2)), ((0, 0), (0, 0), (0, E - levels)))
-    part = call(local_kernel, part_shape, queries, lin_keys, lin_values, cls, tab)
-    from_zh = swap(call(total_kernel, copies, from_zl), "zh")
-    seg_row = jnp.pad(seg_ids.astype(BF16)[None], ((0, 15), (0, 2 * KVH * E - TILE)))
-    packed = jnp.concatenate([jnp.concatenate([win_keys, win_values], axis=1), seg_row], axis=0)
+    seg_rows = jnp.broadcast_to(seg_ids[None], (8, TILE))
+
+    sum1 = span_state(lin_keys, lin_values)
+    from_zl = swap(sum1, "zl")
+    part = call(local_kernel, part_shape, queries, lin_keys, lin_values, cls, tab, after=(sum1,))
+
+    sum4 = call(total_kernel, copies, from_zl, after=(part,))
+    from_zh = swap(sum4, "zh")
+    packed = call(pack_kernel, sds((TILE + 16, 2 * KVH * E), BF16), win_keys, win_values, seg_rows, after=(sum4,))
     flat = ("x", "zh", "zl", "head")
     rims = [lax.ppermute(packed, flat, [(i, i + d) for i in range(512 - d)]) for d in (1, 2)]
     part = call(
-        functools.partial(level_kernel, "zl", 5), part_shape, from_zl, queries, cls, tab, part, aliases={4: 0}
+        functools.partial(level_kernel, "zl", 5),
+        part_shape,
+        from_zl,
+        queries,
+        cls,
+        tab,
+        part,
+        after=(packed,),
+        aliases={4: 0},
     )
-    from_x = swap(call(total_kernel, copies, from_zh), "x")
+
+    sum16 = call(total_kernel, copies, from_zh, after=(part, rims[0], rims[1]))
+    from_x = swap(sum16, "x")
     part = call(
-        functools.partial(level_kernel, "zh", 7), part_shape, from_zh, queries, cls, tab, part, aliases={4: 0}
+        functools.partial(level_kernel, "zh", 7),
+        part_shape,
+        from_zh,
+        queries,
+        cls,
+        tab,
+        part,
+        after=(sum16,),
+        aliases={4: 0},
     )
     mixed, gated = call(
         functools.partial(final_kernel, "x", 9),
@@ -279,16 +347,7 @@
         part,
     )
     token_q = swap(gated, "head")
-    out = call(
-        window_kernel,
-        sds((TILE, H * E), BF16),
-        token_q,
-        win_keys,
-        win_values,
-        jnp.broadcast_to(seg_ids[None], (8, TILE)),
-        rims[0],
-        rims[1],
-    )
+    out = call(window_kernel, sds((TILE, H * E), BF16), token_q, win_keys, win_values, seg_rows, rims[0], rims[1])
     return mixed, out
 
 

time: 94.1 us -> 90.5 us (0.962)
  the two profiles are of different devices: /device:TPU:3 before, /device:TPU:1 now
where the time goes in v2:
time: 90.5 us; the launch traced here: 90 us
  starting transfers between devices  47 us (52%)
  Pallas kernels  17 us (19%)
  blocking collectives  17 us (19%)
  waiting for transfers between devices  6.52 us (7%)
  local copies, waits for them, and re-layouts  1.73 us (2%)
    all_to_all x3, starting transfers between devices, swap(): return lax.all_to_all(value, axis, split_axis=0, concat_axis=0, tiled=True)  37.7 us
    all_to_all x1, blocking collectives, swap(): return lax.all_to_all(value, axis, split_axis=0, concat_axis=0, tiled=True)  17 us
    pallas_call x8, Pallas kernels, call(): pl.pallas_call(body, out_shape=out, in_specs=[vmem] * count + [pl.BlockSp...  14.2 us
    ppermute x2, starting transfers between devices, local(): lax.ppermute(packed, flat, [(i, i + d) for i in range(512 - d)])  9.31 us
    all_to_all x3, waiting for transfers between devices, swap(): return lax.all_to_all(value, axis, split_axis=0, concat_axis=0, tiled=True)  4.13 us
    pallas_call x1, Pallas kernels, span_state(): pl.pallas_call(state_kernel, out_shape=jax.ShapeDtypeStruct((4, ROWS, E),...  2.76 us
    ppermute x2, waiting for transfers between devices, local(): lax.ppermute(packed, flat, [(i, i + d) for i in range(512 - d)])  2.39 us
  transfers between devices with their start and end apart: 5, of which 2 were waited for; matrix products, arithmetic and copies ran while one was open for 0% of the time, Pallas kernels for 9%

profile of v2, /device:TPU:1, one launch (start us, length us, event | category | flops | bytes accessed | tf_op | source)
XLA Modules:
  0.0 90.0 jit_solution(6211216205529826775)
XLA Ops:
  0.6 0.0 copy-start.2
  0.6 0.0 copy-start.3
  0.6 2.8 %shard_map.95.refs_5_ = bf16[4,272,128]{2,1,0:T(8,128)(2,1)} custom-call(bf16[1024,256]{1,0:T(8,128)(2,1)} %refs_1_.6, bf16[1024,256]{1,0:T(8,128)(2,1)} %refs_2_.2), custom_call_target="tpu_custom_call" | custom-call | tf_op jit(solution)/shard_map/pallas_call | solution.py:272
  3.4 0.0 copy-start.7
  3.4 0.0 copy-start
  3.4 6.6 %all-to-all-start = ((bf16[4,272,128]{2,1,0:T(8,128)(2,1)}), bf16[4,272,128]{2,1,0:T(8,128)(2,1)S(1)}, u32[]{:S(2)}, u32[]{:S(2)}) async-start(bf16[4,272,128]{2,1,0:T(8,128)(2,1)} %shard_map.95.refs_5_), calls=%async_computation | async-start | bytes 557056 | tf_op jit(solution)/shard_map/all_to_all | solution.py:294
  10.0 0.0 copy-done.7
  10.0 0.1 copy.12
  10.1 0.0 copy-start.6
  10.1 0.0 copy-done.2
  10.1 0.0 copy-done.3
  10.1 0.0 copy-done
  10.1 0.7 copy-done.6
  10.8 0.0 copy-start.1
  10.8 1.0 %copy-done.1 = bf16[4,272,128]{2,1,0:T(8,128)(2,1)S(1)} copy-done((bf16[4,272,128]{2,1,0:T(8,128)(2,1)S(1)}, bf16[4,272,128]{2,1,0:T(8,128)(2,1)}, u32[]{:S(2)}) %copy-start.1) | copy-done | bytes 278552
  11.8 5.3 %shard_map.96.refs_1_.refs_4_ = f32[1024,256]{1,0:T(8,128)S(1)} custom-call(bf16[1024,256]{1,0:T(8,128)(2,1)S(1)} %copy-done, bf16[1024,256]{1,0:T(8,128)(2,1)S(1)} %copy-done.2, bf16[1024,256]{1,0:T(8,128)(2,1)S(1)} %copy-done.3, s32[8,128]{1,0:T(8,128)S(1)} %bitcast.2, f32[2,16,128]{2,1,0:T(8,128)S(1)} %pad.4.refs_4_.refs_3_, ...), custom_call_target="tpu_custom_call" | custom-call | tf_op jit(solution)/shard_map/pallas_call | solution.py:261
  17.0 0.0 all-to-all-done.refs_0_
  17.0 0.8 shard_map.97.refs_3_
  17.8 0.0 copy-start.8
  17.8 0.0 copy-start.4
  17.8 0.0 copy-start.5
  17.8 13.5 %all-to-all-start.1 = ((bf16[4,272,128]{2,1,0:T(8,128)(2,1)}), bf16[4,272,128]{2,1,0:T(8,128)(2,1)S(1)}, u32[]{:S(2)}, u32[]{:S(2)}) async-start(bf16[4,272,128]{2,1,0:T(8,128)(2,1)} %shard_map.97.refs_3_), calls=%async_computation.1 | async-start | bytes 557056 | tf_op jit(solution)/shard_map/all_to_all | solution.py:294
  31.3 0.0 copy-done.8
  31.3 0.0 copy-done.4
  31.3 0.0 copy-done.5
  31.3 3.2 %collective-permute-start.1 = (bf16[144,1024]{1,0:T(8,128)(2,1)S(1)}, bf16[144,1024]{1,0:T(8,128)(2,1)S(1)}, u32[]{:S(2)}, u32[]{:S(2)}) collective-permute-start(bf16[144,1024]{1,0:T(8,128)(2,1)S(1)} %shard_map.98.refs_5_), channel_id=1, source_target_pairs={{0,2},{1,3},{2,4},{3,5},{4,6},{5,7},{6,8},{7,9},{8,10},{9,11},{10,... | collective-permute-start | bytes 884744 | tf_op jit(solution)/shard_map/ppermute | solution.py:314
  34.6 6.1 %collective-permute-start = (bf16[144,1024]{1,0:T(8,128)(2,1)S(1)}, bf16[144,1024]{1,0:T(8,128)(2,1)S(1)}, u32[]{:S(2)}, u32[]{:S(2)}) collective-permute-start(bf16[144,1024]{1,0:T(8,128)(2,1)S(1)} %shard_map.98.refs_5_), channel_id=1, source_target_pairs={{0,1},{1,2},{2,3},{3,4},{4,5},{5,6},{6,7},{7,8},{8,9},{9,10},{10,1... | collective-permute-start | bytes 884744 | tf_op jit(solution)/shard_map/ppermute | solution.py:314
  40.7 1.5 %shard_map.99.refs_1_.refs_4_ = f32[1024,256]{1,0:T(8,128)S(1)} custom-call(bf16[4,272,128]{2,1,0:T(8,128)(2,1)S(1)} %all-to-all-done.refs_0_, bf16[1024,256]{1,0:T(8,128)(2,1)S(1)} %copy-done, s32[8,128]{1,0:T(8,128)S(1)} %bitcast.3, f32[2,16,128]{2,1,0:T(8,128)S(1)} %pad.4.refs_4_.refs_3_, ...), custom_call_target="tpu_custom_call", output_to_operand_aliasing={{}: (4, {})} | custom-call | tf_op jit(solution)/shard_map/pallas_call | solution.py:261
  42.2 0.0 collective-permute-done.1.refs_3_.refs_5_
  42.2 2.4 %collective-permute-done.refs_2_.refs_4_ = bf16[144,1024]{1,0:T(8,128)(2,1)S(1)} collective-permute-done((bf16[144,1024]{1,0:T(8,128)(2,1)S(1)}, bf16[144,1024]{1,0:T(8,128)(2,1)S(1)}, u32[]{:S(2)}, u32[]{:S(2)}) %collective-permute-start) | collective-permute-done | bytes 294944 | tf_op jit(solution)/shard_map/ppermute | solution.py:314
  44.6 0.0 all-to-all-done.1.refs_0_
  44.6 0.8 shard_map.100.refs_5_
  45.3 17.6 %all-to-all-start.2 = ((bf16[4,272,128]{2,1,0:T(8,128)(2,1)}), bf16[4,272,128]{2,1,0:T(8,128)(2,1)S(1)}, u32[]{:S(2)}, u32[]{:S(2)}) async-start(bf16[4,272,128]{2,1,0:T(8,128)(2,1)} %shard_map.100.refs_5_), calls=%async_computation.2 | async-start | bytes 557056 | tf_op jit(solution)/shard_map/all_to_all | solution.py:294
  62.9 1.5 %shard_map.101.refs_4_ = f32[1024,256]{1,0:T(8,128)S(1)} custom-call(bf16[4,272,128]{2,1,0:T(8,128)(2,1)S(1)} %all-to-all-done.1.refs_0_, bf16[1024,256]{1,0:T(8,128)(2,1)S(1)} %copy-done, s32[8,128]{1,0:T(8,128)S(1)} %bitcast.4, f32[2,16,128]{2,1,0:T(8,128)S(1)} %pad.4.refs_4_.refs_3_, ...), custom_call_target="tpu_custom_call", output_to_operand_aliasing={{}: (4, {})} | custom-call | tf_op jit(solution)/shard_map/pallas_call | solution.py:261
  64.4 4.1 %all-to-all-done.2.refs_0_ = bf16[4,272,128]{2,1,0:T(8,128)(2,1)S(1)} async-done(((bf16[4,272,128]{2,1,0:T(8,128)(2,1)}), bf16[4,272,128]{2,1,0:T(8,128)(2,1)S(1)}, u32[]{:S(2)}, u32[]{:S(2)}) %all-to-all-start.2) | async-done | bytes 278560 | tf_op jit(solution)/shard_map/all_to_all | solution.py:294
  68.6 2.1 %shard_map.102 = (bf16[1024,256]{1,0:T(8,128)(2,1)}, bf16[8,128,256]{2,1,0:T(8,128)(2,1)S(1)}) custom-call(bf16[4,272,128]{2,1,0:T(8,128)(2,1)S(1)} %all-to-all-done.2.refs_0_, bf16[1024,256]{1,0:T(8,128)(2,1)S(1)} %copy-done, s32[8,128]{1,0:T(8,128)S(1)} %bitcast.5, f32[2,16,128]{2,1,0:T(8,128)S(1)} %pad.4.refs_4_.refs_3_, f32[1024,256]{1,0:T(8,128)S(1)} %shard_map.101.refs_4_), custom_call_target="tpu_custom_call" | custom-call | tf_op jit(solution)/shard_map/pallas_call | solution.py:261
  70.6 17.0 %all_to_all.20.refs_0_ = bf16[8,128,256]{2,1,0:T(8,128)(2,1)S(1)} all-to-all(bf16[8,128,256]{2,1,0:T(8,128)(2,1)S(1)} %get-tuple-element.5), channel_id=1, replica_groups=mesh['x'=4,'zh'=4,'zl'=4,'head'=8] {'head'}, dimensions={0} | all-to-all | bytes 1048576 | tf_op jit(solution)/shard_map/all_to_all | solution.py:294
  87.6 2.4 %shard_map.103 = bf16[128,2048]{1,0:T(8,128)(2,1)} custom-call(bf16[8,128,256]{2,1,0:T(8,128)(2,1)S(1)} %all_to_all.20.refs_0_, bf16[128,512]{1,0:T(8,128)(2,1)S(1)} %copy-done.4, bf16[128,512]{1,0:T(8,128)(2,1)S(1)} %copy-done.5, s32[8,128]{1,0:T(8,128)S(1)} %broadcast_in_dim.2.refs_2_.refs_3_, bf16[144,1024]{1,0:T(8,128)(2,1)S(1)} %collective-permute-done.refs_2_.refs_4_, ...), custom_call_target="tpu_custom_call" | custom-call | tf_op jit(solution)/shard_map/pallas_call | solution.py:261
  (3 shorter events, 0.0 us)
Async XLA Ops:
  0.6 9.5 %copy-start.2 = (bf16[1024,256]{1,0:T(8,128)(2,1)S(1)}, bf16[1024,256]{1,0:T(8,128)(2,1)}, u32[]{:S(2)}) copy-start(bf16[1024,256]{1,0:T(8,128)(2,1)} %refs_1_.6) | copy-start | bytes 1572868
  0.6 9.5 %copy-start.3 = (bf16[1024,256]{1,0:T(8,128)(2,1)S(1)}, bf16[1024,256]{1,0:T(8,128)(2,1)}, u32[]{:S(2)}) copy-start(bf16[1024,256]{1,0:T(8,128)(2,1)} %refs_2_.2) | copy-start | bytes 1572868
  3.4 6.6 %copy-start.7 = (f32[16,2,11]{0,1,2:T(2,128)S(1)}, f32[16,2,11]{0,1,2:T(2,128)}, u32[]{:S(2)}) copy-start(f32[16,2,11]{0,1,2:T(2,128)} %param.12) | copy-start | bytes 4228
  3.4 6.7 %copy-start = (bf16[1024,256]{1,0:T(8,128)(2,1)S(1)}, bf16[1024,256]{1,0:T(8,128)(2,1)}, u32[]{:S(2)}) copy-start(bf16[1024,256]{1,0:T(8,128)(2,1)} %refs_1_.10) | copy-start | bytes 1572868
  3.4 13.6 %all-to-all-start = ((bf16[4,272,128]{2,1,0:T(8,128)(2,1)}), bf16[4,272,128]{2,1,0:T(8,128)(2,1)S(1)}, u32[]{:S(2)}, u32[]{:S(2)}) async-start(bf16[4,272,128]{2,1,0:T(8,128)(2,1)} %shard_map.95.refs_5_), calls=%async_computation | async-start | bytes 557056 | tf_op jit(solution)/shard_map/all_to_all | solution.py:294
  10.1 0.7 copy-start.6
  10.8 1.0 %copy-start.1 = (bf16[4,272,128]{2,1,0:T(8,128)(2,1)S(1)}, bf16[4,272,128]{2,1,0:T(8,128)(2,1)}, u32[]{:S(2)}) copy-start(bf16[4,272,128]{2,1,0:T(8,128)(2,1)} %shard_map.95.refs_5_) | copy-start | bytes 835588
  17.8 13.5 %copy-start.8 = (s32[128]{0:T(128)S(1)}, s32[128]{0:T(128)}, u32[]{:S(2)}) copy-start(s32[128]{0:T(128)} %param.15) | copy-start | bytes 1540
  17.8 13.5 %copy-start.4 = (bf16[128,512]{1,0:T(8,128)(2,1)S(1)}, bf16[128,512]{1,0:T(8,128)(2,1)}, u32[]{:S(2)}) copy-start(bf16[128,512]{1,0:T(8,128)(2,1)} %refs_1_.11) | copy-start | bytes 393220
  17.8 13.5 %copy-start.5 = (bf16[128,512]{1,0:T(8,128)(2,1)S(1)}, bf16[128,512]{1,0:T(8,128)(2,1)}, u32[]{:S(2)}) copy-start(bf16[128,512]{1,0:T(8,128)(2,1)} %refs_2_.3) | copy-start | bytes 393220
  17.8 26.8 %all-to-all-start.1 = ((bf16[4,272,128]{2,1,0:T(8,128)(2,1)}), bf16[4,272,128]{2,1,0:T(8,128)(2,1)S(1)}, u32[]{:S(2)}, u32[]{:S(2)}) async-start(bf16[4,272,128]{2,1,0:T(8,128)(2,1)} %shard_map.97.refs_3_), calls=%async_computation.1 | async-start | bytes 557056 | tf_op jit(solution)/shard_map/all_to_all | solution.py:294
  31.3 10.8 %collective-permute-start.1 = (bf16[144,1024]{1,0:T(8,128)(2,1)S(1)}, bf16[144,1024]{1,0:T(8,128)(2,1)S(1)}, u32[]{:S(2)}, u32[]{:S(2)}) collective-permute-start(bf16[144,1024]{1,0:T(8,128)(2,1)S(1)} %shard_map.98.refs_5_), channel_id=1, source_target_pairs={{0,2},{1,3},{2,4},{3,5},{4,6},{5,7},{6,8},{7,9},{8,10},{9,11},{10,... | collective-permute-start | bytes 884744 | tf_op jit(solution)/shard_map/ppermute | solution.py:314
  34.6 10.0 %collective-permute-start = (bf16[144,1024]{1,0:T(8,128)(2,1)S(1)}, bf16[144,1024]{1,0:T(8,128)(2,1)S(1)}, u32[]{:S(2)}, u32[]{:S(2)}) collective-permute-start(bf16[144,1024]{1,0:T(8,128)(2,1)S(1)} %shard_map.98.refs_5_), channel_id=1, source_target_pairs={{0,1},{1,2},{2,3},{3,4},{4,5},{5,6},{6,7},{7,8},{8,9},{9,10},{10,1... | collective-permute-start | bytes 884744 | tf_op jit(solution)/shard_map/ppermute | solution.py:314
  45.3 23.2 %all-to-all-start.2 = ((bf16[4,272,128]{2,1,0:T(8,128)(2,1)}), bf16[4,272,128]{2,1,0:T(8,128)(2,1)S(1)}, u32[]{:S(2)}, u32[]{:S(2)}) async-start(bf16[4,272,128]{2,1,0:T(8,128)(2,1)} %shard_map.100.refs_5_), calls=%async_computation.2 | async-start | bytes 557056 | tf_op jit(solution)/shard_map/all_to_all | solution.py:294

commit v3 on v2

--- a/solution.py
+++ b/solution.py
@@ -15,7 +15,7 @@
 HEADS = 2
 TOK = 1024
 TILE = 128
-CHUNK = 256
+CHUNK = 512
 CHUNKS = TOK // CHUNK
 SUMS = HEADS * E
 ROWS = SUMS + 16
@@ -290,6 +290,18 @@
     out_ref[TILE:, :TILE] = jnp.broadcast_to(seg_ref[0:1, :].astype(F32), (16, TILE)).astype(BF16)
 
 
+def pick_kernel(own_ref, got_ref, out_ref):
+    first = lax.rem(lax.axis_index("head"), 2) == 0
+
+    @pl.when(first)
+    def _():
+        out_ref[...] = own_ref[...]
+
+    @pl.when(jnp.logical_not(first))
+    def _():
+        out_ref[...] = got_ref[...]
+
+
 def swap(value, axis):
     return lax.all_to_all(value, axis, split_axis=0, concat_axis=0, tiled=True)
 
@@ -305,27 +317,19 @@
 
     sum1 = span_state(lin_keys, lin_values)
     from_zl = swap(sum1, "zl")
-    part = call(local_kernel, part_shape, queries, lin_keys, lin_values, cls, tab, after=(sum1,))
-
-    sum4 = call(total_kernel, copies, from_zl, after=(part,))
+    sum4 = call(total_kernel, copies, from_zl)
     from_zh = swap(sum4, "zh")
-    packed = call(pack_kernel, sds((TILE + 16, 2 * KVH * E), BF16), win_keys, win_values, seg_rows, after=(sum4,))
+    part = call(local_kernel, part_shape, queries, lin_keys, lin_values, cls, tab, after=(sum4,))
+    part = call(
+        functools.partial(level_kernel, "zl", 5), part_shape, from_zl, queries, cls, tab, part, aliases={4: 0}
+    )
+
+    sum16 = call(total_kernel, copies, from_zh, after=(part,))
+    from_x = swap(sum16, "x")
+    rim = sds((TILE + 16, 2 * KVH * E), BF16)
+    packed = call(pack_kernel, rim, win_keys, win_values, seg_rows, after=(sum16,))
     flat = ("x", "zh", "zl", "head")
-    rims = [lax.ppermute(packed, flat, [(i, i + d) for i in range(512 - d)]) for d in (1, 2)]
-    part = call(
-        functools.partial(level_kernel, "zl", 5),
-        part_shape,
-        from_zl,
-        queries,
-        cls,
-        tab,
-        part,
-        after=(packed,),
-        aliases={4: 0},
-    )
-
-    sum16 = call(total_kernel, copies, from_zh, after=(part, rims[0], rims[1]))
-    from_x = swap(sum16, "x")
+    rim2 = lax.ppermute(packed, flat, [(i, i + 2) for i in range(510)])
     part = call(
         functools.partial(level_kernel, "zh", 7),
         part_shape,
@@ -334,7 +338,7 @@
         cls,
         tab,
         part,
-        after=(sum16,),
+        after=(packed,),
         aliases={4: 0},
     )
     mixed, gated = call(
@@ -347,7 +351,9 @@
         part,
     )
     token_q = swap(gated, "head")
-    out = call(window_kernel, sds((TILE, H * E), BF16), token_q, win_keys, win_values, seg_rows, rims[0], rims[1])
+    picked = call(pick_kernel, rim, packed, rim2, after=(gated,))
+    rim1 = lax.ppermute(picked, "head", [(i, i ^ 1) for i in range(8)])
+    out = call(window_kernel, sds((TILE, H * E), BF16), token_q, win_keys, win_values, seg_rows, rim1, rim2)
     return mixed, out
 
 

time: 90.5 us -> 82.4 us (0.910)
  the two profiles are of different devices: /device:TPU:1 before, /device:TPU:32 now
where the time goes in v3:
time: 82.4 us; the launch traced here: 81.9 us
  starting transfers between devices  26.3 us (32%)
  waiting for transfers between devices  21.8 us (26%)
  Pallas kernels  16.9 us (21%)
  blocking collectives  15.4 us (19%)
    all_to_all x3, waiting for transfers between devices, swap(): return lax.all_to_all(value, axis, split_axis=0, concat_axis=0, tiled=True)  20.6 us
    all_to_all x3, starting transfers between devices, swap(): return lax.all_to_all(value, axis, split_axis=0, concat_axis=0, tiled=True)  20.4 us
    all_to_all x1, blocking collectives, swap(): return lax.all_to_all(value, axis, split_axis=0, concat_axis=0, tiled=True)  15.4 us
    pallas_call x9, Pallas kernels, call(): pl.pallas_call(body, out_shape=out, in_specs=[vmem] * count + [pl.BlockSp...  14.5 us
    ppermute x1, starting transfers between devices, local(): rim2 = lax.ppermute(packed, flat, [(i, i + 2) for i in range(510)])  3.48 us
    ppermute x1, starting transfers between devices, local(): rim1 = lax.ppermute(picked, 'head', [(i, i ^ 1) for i in range(8)])  2.39 us
    pallas_call x1, Pallas kernels, span_state(): pl.pallas_call(state_kernel, out_shape=jax.ShapeDtypeStruct((4, ROWS, E),...  2.35 us
  transfers between devices with their start and end apart: 5, of which 4 were waited for; matrix products, arithmetic and copies ran while one was open for 0% of the time, Pallas kernels for 13%

profile of v3, /device:TPU:32, one launch (start us, length us, event | category | flops | bytes accessed | tf_op | source)
XLA Modules:
  0.0 81.9 jit_solution(10299302551747129752)
XLA Ops:
  0.6 2.3 %shard_map.95 = bf16[4,272,128]{2,1,0:T(8,128)(2,1)} custom-call(bf16[1024,256]{1,0:T(8,128)(2,1)} %refs_1_.6, bf16[1024,256]{1,0:T(8,128)(2,1)} %refs_2_.2), custom_call_target="tpu_custom_call" | custom-call | tf_op jit(solution)/shard_map/pallas_call | solution.py:272
  3.0 0.0 copy-start.2
  3.0 15.4 %all_to_all.20.refs_0_ = bf16[4,272,128]{2,1,0:T(8,128)(2,1)S(1)} all-to-all(bf16[4,272,128]{2,1,0:T(8,128)(2,1)} %shard_map.95), channel_id=1, replica_groups=mesh['x'=4,'zh'=4,'zl'=4,'head'=8] {'zl'}, dimensions={0} | all-to-all | bytes 557056 | tf_op jit(solution)/shard_map/all_to_all | solution.py:306
  18.4 0.0 copy-start
  18.4 0.0 copy-start.1
  18.4 0.8 shard_map.96.refs_5_
  19.1 0.0 copy-start.6
  19.1 11.5 %all-to-all-start.1 = ((bf16[4,272,128]{2,1,0:T(8,128)(2,1)}), bf16[4,272,128]{2,1,0:T(8,128)(2,1)S(1)}, u32[]{:S(2)}, u32[]{:S(2)}) async-start(bf16[4,272,128]{2,1,0:T(8,128)(2,1)} %shard_map.96.refs_5_), calls=%async_computation.1 | async-start | bytes 557056 | tf_op jit(solution)/shard_map/all_to_all | solution.py:306
  30.6 0.0 copy-done.6
  30.6 0.1 copy.12
  30.7 0.0 copy-start.5
  30.7 0.0 copy-done.2
  30.7 0.0 copy-done
  30.8 0.0 copy-done.1
  30.8 0.7 copy-done.5
  31.4 5.3 %shard_map.97.refs_4_ = f32[1024,256]{1,0:T(8,128)S(1)} custom-call(bf16[1024,256]{1,0:T(8,128)(2,1)S(1)} %copy-done, bf16[1024,256]{1,0:T(8,128)(2,1)S(1)} %copy-done.1, bf16[1024,256]{1,0:T(8,128)(2,1)S(1)} %copy-done.2, s32[8,128]{1,0:T(8,128)S(1)} %bitcast.2, f32[2,16,128]{2,1,0:T(8,128)S(1)} %pad.4.refs_4_.refs_3_, bf16[4,272,128]{2,1,0:T(8,128)(2,1)} %shard_map.96.refs_5_), custom_call_target="tpu_custom_call" | custom-call | tf_op jit(solution)/shard_map/pallas_call | solution.py:261
  36.7 1.5 %shard_map.98.refs_1_.refs_4_ = f32[1024,256]{1,0:T(8,128)S(1)} custom-call(bf16[4,272,128]{2,1,0:T(8,128)(2,1)S(1)} %all_to_all.20.refs_0_, bf16[1024,256]{1,0:T(8,128)(2,1)S(1)} %copy-done, s32[8,128]{1,0:T(8,128)S(1)} %bitcast.3, f32[2,16,128]{2,1,0:T(8,128)S(1)} %pad.4.refs_4_.refs_3_, ...), custom_call_target="tpu_custom_call", output_to_operand_aliasing={{}: (4, {})} | custom-call | tf_op jit(solution)/shard_map/pallas_call | solution.py:261
  38.2 12.2 %all-to-all-done.1.refs_0_ = bf16[4,272,128]{2,1,0:T(8,128)(2,1)S(1)} async-done(((bf16[4,272,128]{2,1,0:T(8,128)(2,1)}), bf16[4,272,128]{2,1,0:T(8,128)(2,1)S(1)}, u32[]{:S(2)}, u32[]{:S(2)}) %all-to-all-start.1) | async-done | bytes 278560 | tf_op jit(solution)/shard_map/all_to_all | solution.py:306
  50.4 0.8 shard_map.99.refs_3_
  51.2 0.0 copy-start.7
  51.2 0.0 copy-start.3
  51.2 0.0 copy-start.4
  51.2 4.4 %all-to-all-start.2 = ((bf16[4,272,128]{2,1,0:T(8,128)(2,1)}), bf16[4,272,128]{2,1,0:T(8,128)(2,1)S(1)}, u32[]{:S(2)}, u32[]{:S(2)}) async-start(bf16[4,272,128]{2,1,0:T(8,128)(2,1)} %shard_map.99.refs_3_), calls=%async_computation.2 | async-start | bytes 557056 | tf_op jit(solution)/shard_map/all_to_all | solution.py:306
  55.6 0.0 copy-done.7
  55.6 0.0 copy-done.3
  55.6 0.0 copy-done.4
  55.6 3.5 %collective-permute-start = (bf16[144,1024]{1,0:T(8,128)(2,1)S(1)}, bf16[144,1024]{1,0:T(8,128)(2,1)S(1)}, u32[]{:S(2)}, u32[]{:S(2)}) collective-permute-start(bf16[144,1024]{1,0:T(8,128)(2,1)S(1)} %shard_map.100.refs_5_.refs_0_), channel_id=1, source_target_pairs={{0,2},{1,3},{2,4},{3,5},{4,6},{5,7},{6,8},{7,9},{8,10},{9,11},{10,... | collective-permute-start | bytes 884744 | tf_op jit(solution)/shard_map/ppermute | solution.py:332
  59.1 1.5 %shard_map.101.refs_4_ = f32[1024,256]{1,0:T(8,128)S(1)} custom-call(bf16[4,272,128]{2,1,0:T(8,128)(2,1)S(1)} %all-to-all-done.1.refs_0_, bf16[1024,256]{1,0:T(8,128)(2,1)S(1)} %copy-done, s32[8,128]{1,0:T(8,128)S(1)} %bitcast.4, f32[2,16,128]{2,1,0:T(8,128)S(1)} %pad.4.refs_4_.refs_3_, ...), custom_call_target="tpu_custom_call", output_to_operand_aliasing={{}: (4, {})} | custom-call | tf_op jit(solution)/shard_map/pallas_call | solution.py:261
  60.6 1.7 %all-to-all-done.2.refs_0_ = bf16[4,272,128]{2,1,0:T(8,128)(2,1)S(1)} async-done(((bf16[4,272,128]{2,1,0:T(8,128)(2,1)}), bf16[4,272,128]{2,1,0:T(8,128)(2,1)S(1)}, u32[]{:S(2)}, u32[]{:S(2)}) %all-to-all-start.2) | async-done | bytes 278560 | tf_op jit(solution)/shard_map/all_to_all | solution.py:306
  62.4 2.3 %shard_map.102 = (bf16[1024,256]{1,0:T(8,128)(2,1)}, bf16[8,128,256]{2,1,0:T(8,128)(2,1)}) custom-call(bf16[4,272,128]{2,1,0:T(8,128)(2,1)S(1)} %all-to-all-done.2.refs_0_, bf16[1024,256]{1,0:T(8,128)(2,1)S(1)} %copy-done, s32[8,128]{1,0:T(8,128)S(1)} %bitcast.5, f32[2,16,128]{2,1,0:T(8,128)S(1)} %pad.4.refs_4_.refs_3_, f32[1024,256]{1,0:T(8,128)S(1)} %shard_map.101.refs_4_), custom_call_target="tpu_custom_call" | custom-call | tf_op jit(solution)/shard_map/pallas_call | solution.py:261
  64.6 4.5 %all-to-all-start.3 = ((bf16[8,128,256]{2,1,0:T(8,128)(2,1)}), bf16[8,128,256]{2,1,0:T(8,128)(2,1)S(1)}, u32[]{:S(2)}, u32[]{:S(2)}) async-start(bf16[8,128,256]{2,1,0:T(8,128)(2,1)} %get-tuple-element.5.refs_2_), calls=%async_computation.3 | async-start | bytes 1048576 | tf_op jit(solution)/shard_map/all_to_all | solution.py:306
  69.1 0.0 collective-permute-done.refs_1_.refs_5_
  69.2 2.4 %collective-permute-start.1 = (bf16[144,1024]{1,0:T(8,128)(2,1)S(1)}, bf16[144,1024]{1,0:T(8,128)(2,1)S(1)}, u32[]{:S(2)}, u32[]{:S(2)}) collective-permute-start(bf16[144,1024]{1,0:T(8,128)(2,1)S(1)} %shard_map.103), channel_id=1, source_target_pairs={{0,1},{1,0},{2,3},{3,2},{4,5},{5,4},{6,7},{7,6},{8,9},{9,8},{10,11... | collective-permute-start | bytes 884744 | tf_op jit(solution)/shard_map/ppermute | solution.py:355
  71.6 1.2 %collective-permute-done.1.refs_4_ = bf16[144,1024]{1,0:T(8,128)(2,1)S(1)} collective-permute-done((bf16[144,1024]{1,0:T(8,128)(2,1)S(1)}, bf16[144,1024]{1,0:T(8,128)(2,1)S(1)}, u32[]{:S(2)}, u32[]{:S(2)}) %collective-permute-start.1) | collective-permute-done | bytes 294944 | tf_op jit(solution)/shard_map/ppermute | solution.py:355
  72.7 6.7 %all-to-all-done.3.refs_0_ = bf16[8,128,256]{2,1,0:T(8,128)(2,1)S(1)} async-done(((bf16[8,128,256]{2,1,0:T(8,128)(2,1)}), bf16[8,128,256]{2,1,0:T(8,128)(2,1)S(1)}, u32[]{:S(2)}, u32[]{:S(2)}) %all-to-all-start.3) | async-done | bytes 524320 | tf_op jit(solution)/shard_map/all_to_all | solution.py:306
  79.5 2.4 %shard_map.104 = bf16[128,2048]{1,0:T(8,128)(2,1)} custom-call(bf16[8,128,256]{2,1,0:T(8,128)(2,1)S(1)} %all-to-all-done.3.refs_0_, bf16[128,512]{1,0:T(8,128)(2,1)S(1)} %copy-done.3, bf16[128,512]{1,0:T(8,128)(2,1)S(1)} %copy-done.4, s32[8,128]{1,0:T(8,128)S(1)} %broadcast_in_dim.2.refs_2_.refs_3_, bf16[144,1024]{1,0:T(8,128)(2,1)S(1)} %collective-permute-done.1.refs_4_, ...), custom_call_target="tpu_custom_call" | custom-call | tf_op jit(solution)/shard_map/pallas_call | solution.py:261
  (4 shorter events, 0.1 us)
Async XLA Ops:
  3.0 27.8 %copy-start.2 = (bf16[1024,256]{1,0:T(8,128)(2,1)S(1)}, bf16[1024,256]{1,0:T(8,128)(2,1)}, u32[]{:S(2)}) copy-start(bf16[1024,256]{1,0:T(8,128)(2,1)} %refs_2_.2) | copy-start | bytes 1572868
  18.4 12.4 %copy-start = (bf16[1024,256]{1,0:T(8,128)(2,1)S(1)}, bf16[1024,256]{1,0:T(8,128)(2,1)}, u32[]{:S(2)}) copy-start(bf16[1024,256]{1,0:T(8,128)(2,1)} %refs_1_.10) | copy-start | bytes 1572868
  18.4 12.4 %copy-start.1 = (bf16[1024,256]{1,0:T(8,128)(2,1)S(1)}, bf16[1024,256]{1,0:T(8,128)(2,1)}, u32[]{:S(2)}) copy-start(bf16[1024,256]{1,0:T(8,128)(2,1)} %refs_1_.6) | copy-start | bytes 1572868
  19.1 11.5 %copy-start.6 = (f32[16,2,11]{0,1,2:T(2,128)S(1)}, f32[16,2,11]{0,1,2:T(2,128)}, u32[]{:S(2)}) copy-start(f32[16,2,11]{0,1,2:T(2,128)} %param.12) | copy-start | bytes 4228
  19.1 31.3 %all-to-all-start.1 = ((bf16[4,272,128]{2,1,0:T(8,128)(2,1)}), bf16[4,272,128]{2,1,0:T(8,128)(2,1)S(1)}, u32[]{:S(2)}, u32[]{:S(2)}) async-start(bf16[4,272,128]{2,1,0:T(8,128)(2,1)} %shard_map.96.refs_5_), calls=%async_computation.1 | async-start | bytes 557056 | tf_op jit(solution)/shard_map/all_to_all | solution.py:306
  30.7 0.7 copy-start.5
  51.2 4.4 %copy-start.7 = (s32[128]{0:T(128)S(1)}, s32[128]{0:T(128)}, u32[]{:S(2)}) copy-start(s32[128]{0:T(128)} %param.15) | copy-start | bytes 1540
  51.2 4.4 %copy-start.3 = (bf16[128,512]{1,0:T(8,128)(2,1)S(1)}, bf16[128,512]{1,0:T(8,128)(2,1)}, u32[]{:S(2)}) copy-start(bf16[128,512]{1,0:T(8,128)(2,1)} %refs_1_.11) | copy-start | bytes 393220
  51.2 4.4 %copy-start.4 = (bf16[128,512]{1,0:T(8,128)(2,1)S(1)}, bf16[128,512]{1,0:T(8,128)(2,1)}, u32[]{:S(2)}) copy-start(bf16[128,512]{1,0:T(8,128)(2,1)} %refs_2_.3) | copy-start | bytes 393220
  51.2 11.2 %all-to-all-start.2 = ((bf16[4,272,128]{2,1,0:T(8,128)(2,1)}), bf16[4,272,128]{2,1,0:T(8,128)(2,1)S(1)}, u32[]{:S(2)}, u32[]{:S(2)}) async-start(bf16[4,272,128]{2,1,0:T(8,128)(2,1)} %shard_map.99.refs_3_), calls=%async_computation.2 | async-start | bytes 557056 | tf_op jit(solution)/shard_map/all_to_all | solution.py:306
  55.6 13.5 %collective-permute-start = (bf16[144,1024]{1,0:T(8,128)(2,1)S(1)}, bf16[144,1024]{1,0:T(8,128)(2,1)S(1)}, u32[]{:S(2)}, u32[]{:S(2)}) collective-permute-start(bf16[144,1024]{1,0:T(8,128)(2,1)S(1)} %shard_map.100.refs_5_.refs_0_), channel_id=1, source_target_pairs={{0,2},{1,3},{2,4},{3,5},{4,6},{5,7},{6,8},{7,9},{8,10},{9,11},{10,... | collective-permute-start | bytes 884744 | tf_op jit(solution)/shard_map/ppermute | solution.py:332
  64.6 14.8 %all-to-all-start.3 = ((bf16[8,128,256]{2,1,0:T(8,128)(2,1)}), bf16[8,128,256]{2,1,0:T(8,128)(2,1)S(1)}, u32[]{:S(2)}, u32[]{:S(2)}) async-start(bf16[8,128,256]{2,1,0:T(8,128)(2,1)} %get-tuple-element.5.refs_2_), calls=%async_computation.3 | async-start | bytes 1048576 | tf_op jit(solution)/shard_map/all_to_all | solution.py:306
  69.2 3.6 %collective-permute-start.1 = (bf16[144,1024]{1,0:T(8,128)(2,1)S(1)}, bf16[144,1024]{1,0:T(8,128)(2,1)S(1)}, u32[]{:S(2)}, u32[]{:S(2)}) collective-permute-start(bf16[144,1024]{1,0:T(8,128)(2,1)S(1)} %shard_map.103), channel_id=1, source_target_pairs={{0,1},{1,0},{2,3},{3,2},{4,5},{5,4},{6,7},{7,6},{8,9},{9,8},{10,11... | collective-permute-start | bytes 884744 | tf_op jit(solution)/shard_map/ppermute | solution.py:355

commit v4 on v3

--- a/solution.py
+++ b/solution.py
@@ -16,6 +16,9 @@
 TOK = 1024
 TILE = 128
 CHUNK = 512
+PLAIN = (0, 1, 2, 3)
+ZL_ORDER = (1, 2, 0, 3)
+ZH_ORDER = (2, 0, 1, 3)
 CHUNKS = TOK // CHUNK
 SUMS = HEADS * E
 ROWS = SUMS + 16
@@ -165,12 +168,14 @@
             part_ref[rows, cols] = acc
 
 
-def two_levels(axis, first_lane, r_ref, q_ref, cls_ref, tab_ref, part_ref, emit):
+def two_levels(axis, order, first_lane, r_ref, q_ref, cls_ref, tab_ref, part_ref, emit):
     me = lax.axis_index(axis)
     bit0 = (me & 1).astype(F32)
     bit1 = (me >> 1).astype(F32)
-    near = r_ref[jnp.maximum(me - 1, 0)].astype(F32) * bit0
-    wide = (r_ref[0].astype(F32) + r_ref[1].astype(F32)) * bit1
+    place = [order.index(j) for j in range(4)]
+    neighbour = jnp.where(me == 3, place[2], place[0])
+    near = r_ref[neighbour].astype(F32) * bit0
+    wide = (r_ref[place[0]].astype(F32) + r_ref[place[1]].astype(F32)) * bit1
     row_id = lax.broadcasted_iota(jnp.int32, (TILE, E), 0)
     for h in range(HEADS):
         cols = head_cols(h)
@@ -201,21 +206,21 @@
             emit(rows, cols, acc)
 
 
-def level_kernel(axis, first_lane, r_ref, q_ref, cls_ref, tab_ref, part_ref, out_ref):
+def level_kernel(axis, order, first_lane, r_ref, q_ref, cls_ref, tab_ref, part_ref, out_ref):
     def emit(rows, cols, acc):
         out_ref[rows, cols] = acc
 
-    two_levels(axis, first_lane, r_ref, q_ref, cls_ref, tab_ref, part_ref, emit)
-
-
-def final_kernel(axis, first_lane, r_ref, q_ref, cls_ref, tab_ref, part_ref, mixed_ref, gated_ref):
+    two_levels(axis, order, first_lane, r_ref, q_ref, cls_ref, tab_ref, part_ref, emit)
+
+
+def final_kernel(axis, order, first_lane, r_ref, q_ref, cls_ref, tab_ref, part_ref, mixed_ref, gated_ref):
     def emit(rows, cols, acc):
         mixed = acc.astype(BF16)
         mixed_ref[rows, cols] = mixed
         gate = 0.5 + 1.0 / (1.0 + jnp.exp(-mixed.astype(F32)))
         gated_ref[rows.start // TILE, :, cols] = (q_ref[rows, cols].astype(F32) * gate).astype(BF16)
 
-    two_levels(axis, first_lane, r_ref, q_ref, cls_ref, tab_ref, part_ref, emit)
+    two_levels(axis, order, first_lane, r_ref, q_ref, cls_ref, tab_ref, part_ref, emit)
 
 
 def window_kernel(xq_ref, k_ref, v_ref, seg_ref, rim1_ref, rim2_ref, out_ref):
@@ -302,8 +307,9 @@
         out_ref[...] = got_ref[...]
 
 
-def swap(value, axis):
-    return lax.all_to_all(value, axis, split_axis=0, concat_axis=0, tiled=True)
+def swap(value, axis, order=None):
+    groups = None if order is None else [list(order)]
+    return lax.all_to_all(value, axis, split_axis=0, concat_axis=0, axis_index_groups=groups, tiled=True)
 
 
 def local(queries, lin_keys, lin_values, level_class, level_table, win_keys, win_values, seg_ids):
@@ -316,12 +322,12 @@
     seg_rows = jnp.broadcast_to(seg_ids[None], (8, TILE))
 
     sum1 = span_state(lin_keys, lin_values)
-    from_zl = swap(sum1, "zl")
+    from_zl = swap(sum1, "zl", ZL_ORDER)
     sum4 = call(total_kernel, copies, from_zl)
-    from_zh = swap(sum4, "zh")
+    from_zh = swap(sum4, "zh", ZH_ORDER)
     part = call(local_kernel, part_shape, queries, lin_keys, lin_values, cls, tab, after=(sum4,))
     part = call(
-        functools.partial(level_kernel, "zl", 5), part_shape, from_zl, queries, cls, tab, part, aliases={4: 0}
+        functools.partial(level_kernel, "zl", ZL_ORDER, 5), part_shape, from_zl, queries, cls, tab, part, aliases={4: 0}
     )
 
     sum16 = call(total_kernel, copies, from_zh, after=(part,))
@@ -331,7 +337,7 @@
     flat = ("x", "zh", "zl", "head")
     rim2 = lax.ppermute(packed, flat, [(i, i + 2) for i in range(510)])
     part = call(
-        functools.partial(level_kernel, "zh", 7),
+        functools.partial(level_kernel, "zh", ZH_ORDER, 7),
         part_shape,
         from_zh,
         queries,
@@ -342,7 +348,7 @@
         aliases={4: 0},
     )
     mixed, gated = call(
-        functools.partial(final_kernel, "x", 9),
+        functools.partial(final_kernel, "x", PLAIN, 9),
         (sds((TOK, HEADS * E), BF16), sds((8, TILE, HEADS * E), BF16)),
         from_x,
         queries,

time: 82.4 us -> 77.8 us (0.944)
  the two profiles are of different devices: /device:TPU:32 before, /device:TPU:1 now
where the time goes in v4:
time: 77.8 us; the launch traced here: 77.3 us
  starting transfers between devices  32.3 us (42%)
  Pallas kernels  16.8 us (22%)
  waiting for transfers between devices  14.3 us (18%)
  blocking collectives  12.3 us (16%)
    all_to_all x3, starting transfers between devices, swap(): lax.all_to_all(value, axis, split_axis=0, concat_axis=0, axis_index_group...  27.1 us
    pallas_call x9, Pallas kernels, call(): pl.pallas_call(body, out_shape=out, in_specs=[vmem] * count + [pl.BlockSp...  14.5 us
    all_to_all x3, waiting for transfers between devices, swap(): lax.all_to_all(value, axis, split_axis=0, concat_axis=0, axis_index_group...  12.8 us
    all_to_all x1, blocking collectives, swap(): lax.all_to_all(value, axis, split_axis=0, concat_axis=0, axis_index_group...  12.3 us
    ppermute x1, starting transfers between devices, local(): rim2 = lax.ppermute(packed, flat, [(i, i + 2) for i in range(510)])  3.22 us
    pallas_call x1, Pallas kernels, span_state(): pl.pallas_call(state_kernel, out_shape=jax.ShapeDtypeStruct((4, ROWS, E),...  2.35 us
    ppermute x1, starting transfers between devices, local(): rim1 = lax.ppermute(picked, 'head', [(i, i ^ 1) for i in range(8)])  1.94 us
  transfers between devices with their start and end apart: 5, of which 4 were waited for; matrix products, arithmetic and copies ran while one was open for 0% of the time, Pallas kernels for 14%

profile of v4, /device:TPU:1, one launch (start us, length us, event | category | flops | bytes accessed | tf_op | source)
XLA Modules:
  0.0 77.3 jit_solution(5439491623963332367)
XLA Ops:
  0.6 2.3 %shard_map.95 = bf16[4,272,128]{2,1,0:T(8,128)(2,1)} custom-call(bf16[1024,256]{1,0:T(8,128)(2,1)} %refs_1_.6, bf16[1024,256]{1,0:T(8,128)(2,1)} %refs_2_.2), custom_call_target="tpu_custom_call" | custom-call | tf_op jit(solution)/shard_map/pallas_call | solution.py:277
  3.0 0.0 copy-start.2
  3.0 12.3 %all_to_all.20.refs_0_ = bf16[4,272,128]{2,1,0:T(8,128)(2,1)S(1)} all-to-all(bf16[4,272,128]{2,1,0:T(8,128)(2,1)} %shard_map.95), channel_id=1, replica_groups={{8,16,0,24},{9,17,1,25},{10,18,2,26},{11,19,3,27},{12,20,4,28},{13,21,5..., dimensions={0} | all-to-all | bytes 557056 | tf_op jit(solution)/shard_map/all_to_all | solution.py:312
  15.3 0.0 copy-start
  15.3 0.0 copy-start.1
  15.3 0.8 shard_map.96.refs_5_
  16.1 0.0 copy-start.6
  16.1 16.4 %all-to-all-start.1 = ((bf16[4,272,128]{2,1,0:T(8,128)(2,1)}), bf16[4,272,128]{2,1,0:T(8,128)(2,1)S(1)}, u32[]{:S(2)}, u32[]{:S(2)}) async-start(bf16[4,272,128]{2,1,0:T(8,128)(2,1)} %shard_map.96.refs_5_), calls=%async_computation.1 | async-start | bytes 557056 | tf_op jit(solution)/shard_map/all_to_all | solution.py:312
  32.4 0.0 copy-done.6
  32.4 0.1 copy.12
  32.5 0.0 copy-start.5
  32.5 0.0 copy-done.2
  32.6 0.0 copy-done
  32.6 0.0 copy-done.1
  32.6 0.7 copy-done.5
  33.2 5.3 %shard_map.97.refs_4_ = f32[1024,256]{1,0:T(8,128)S(1)} custom-call(bf16[1024,256]{1,0:T(8,128)(2,1)S(1)} %copy-done, bf16[1024,256]{1,0:T(8,128)(2,1)S(1)} %copy-done.1, bf16[1024,256]{1,0:T(8,128)(2,1)S(1)} %copy-done.2, s32[8,128]{1,0:T(8,128)S(1)} %bitcast.2, f32[2,16,128]{2,1,0:T(8,128)S(1)} %pad.4.refs_4_.refs_3_, bf16[4,272,128]{2,1,0:T(8,128)(2,1)} %shard_map.96.refs_5_), custom_call_target="tpu_custom_call" | custom-call | tf_op jit(solution)/shard_map/pallas_call | solution.py:266
  38.5 1.5 %shard_map.98.refs_1_.refs_4_ = f32[1024,256]{1,0:T(8,128)S(1)} custom-call(bf16[4,272,128]{2,1,0:T(8,128)(2,1)S(1)} %all_to_all.20.refs_0_, bf16[1024,256]{1,0:T(8,128)(2,1)S(1)} %copy-done, s32[8,128]{1,0:T(8,128)S(1)} %bitcast.3, f32[2,16,128]{2,1,0:T(8,128)S(1)} %pad.4.refs_4_.refs_3_, ...), custom_call_target="tpu_custom_call", output_to_operand_aliasing={{}: (4, {})} | custom-call | tf_op jit(solution)/shard_map/pallas_call | solution.py:266
  40.0 5.9 %all-to-all-done.1.refs_0_ = bf16[4,272,128]{2,1,0:T(8,128)(2,1)S(1)} async-done(((bf16[4,272,128]{2,1,0:T(8,128)(2,1)}), bf16[4,272,128]{2,1,0:T(8,128)(2,1)S(1)}, u32[]{:S(2)}, u32[]{:S(2)}) %all-to-all-start.1) | async-done | bytes 278560 | tf_op jit(solution)/shard_map/all_to_all | solution.py:312
  46.0 0.8 shard_map.99.refs_3_
  46.7 0.0 copy-start.7
  46.7 0.0 copy-start.3
  46.7 0.0 copy-start.4
  46.7 4.1 %all-to-all-start.2 = ((bf16[4,272,128]{2,1,0:T(8,128)(2,1)}), bf16[4,272,128]{2,1,0:T(8,128)(2,1)S(1)}, u32[]{:S(2)}, u32[]{:S(2)}) async-start(bf16[4,272,128]{2,1,0:T(8,128)(2,1)} %shard_map.99.refs_3_), calls=%async_computation.2 | async-start | bytes 557056 | tf_op jit(solution)/shard_map/all_to_all | solution.py:312
  50.8 0.0 copy-done.7
  50.9 0.0 copy-done.3
  50.9 0.0 copy-done.4
  50.9 3.2 %collective-permute-start = (bf16[144,1024]{1,0:T(8,128)(2,1)S(1)}, bf16[144,1024]{1,0:T(8,128)(2,1)S(1)}, u32[]{:S(2)}, u32[]{:S(2)}) collective-permute-start(bf16[144,1024]{1,0:T(8,128)(2,1)S(1)} %shard_map.100.refs_5_.refs_0_), channel_id=1, source_target_pairs={{0,2},{1,3},{2,4},{3,5},{4,6},{5,7},{6,8},{7,9},{8,10},{9,11},{10,... | collective-permute-start | bytes 884744 | tf_op jit(solution)/shard_map/ppermute | solution.py:338
  54.1 1.5 %shard_map.101.refs_4_ = f32[1024,256]{1,0:T(8,128)S(1)} custom-call(bf16[4,272,128]{2,1,0:T(8,128)(2,1)S(1)} %all-to-all-done.1.refs_0_, bf16[1024,256]{1,0:T(8,128)(2,1)S(1)} %copy-done, s32[8,128]{1,0:T(8,128)S(1)} %bitcast.4, f32[2,16,128]{2,1,0:T(8,128)S(1)} %pad.4.refs_4_.refs_3_, ...), custom_call_target="tpu_custom_call", output_to_operand_aliasing={{}: (4, {})} | custom-call | tf_op jit(solution)/shard_map/pallas_call | solution.py:266
  55.6 0.9 %all-to-all-done.2.refs_0_ = bf16[4,272,128]{2,1,0:T(8,128)(2,1)S(1)} async-done(((bf16[4,272,128]{2,1,0:T(8,128)(2,1)}), bf16[4,272,128]{2,1,0:T(8,128)(2,1)S(1)}, u32[]{:S(2)}, u32[]{:S(2)}) %all-to-all-start.2) | async-done | bytes 278560 | tf_op jit(solution)/shard_map/all_to_all | solution.py:312
  56.5 2.3 %shard_map.102 = (bf16[1024,256]{1,0:T(8,128)(2,1)}, bf16[8,128,256]{2,1,0:T(8,128)(2,1)}) custom-call(bf16[4,272,128]{2,1,0:T(8,128)(2,1)S(1)} %all-to-all-done.2.refs_0_, bf16[1024,256]{1,0:T(8,128)(2,1)S(1)} %copy-done, s32[8,128]{1,0:T(8,128)S(1)} %bitcast.5, f32[2,16,128]{2,1,0:T(8,128)S(1)} %pad.4.refs_4_.refs_3_, f32[1024,256]{1,0:T(8,128)S(1)} %shard_map.101.refs_4_), custom_call_target="tpu_custom_call" | custom-call | tf_op jit(solution)/shard_map/pallas_call | solution.py:266
  58.8 6.6 %all-to-all-start.3 = ((bf16[8,128,256]{2,1,0:T(8,128)(2,1)}), bf16[8,128,256]{2,1,0:T(8,128)(2,1)S(1)}, u32[]{:S(2)}, u32[]{:S(2)}) async-start(bf16[8,128,256]{2,1,0:T(8,128)(2,1)} %get-tuple-element.5.refs_2_), calls=%async_computation.3 | async-start | bytes 1048576 | tf_op jit(solution)/shard_map/all_to_all | solution.py:312
  65.4 0.0 collective-permute-done.refs_1_.refs_5_
  65.4 1.9 %collective-permute-start.1 = (bf16[144,1024]{1,0:T(8,128)(2,1)S(1)}, bf16[144,1024]{1,0:T(8,128)(2,1)S(1)}, u32[]{:S(2)}, u32[]{:S(2)}) collective-permute-start(bf16[144,1024]{1,0:T(8,128)(2,1)S(1)} %shard_map.103), channel_id=1, source_target_pairs={{0,1},{1,0},{2,3},{3,2},{4,5},{5,4},{6,7},{7,6},{8,9},{9,8},{10,11... | collective-permute-start | bytes 884744 | tf_op jit(solution)/shard_map/ppermute | solution.py:361
  67.4 1.5 %collective-permute-done.1.refs_4_ = bf16[144,1024]{1,0:T(8,128)(2,1)S(1)} collective-permute-done((bf16[144,1024]{1,0:T(8,128)(2,1)S(1)}, bf16[144,1024]{1,0:T(8,128)(2,1)S(1)}, u32[]{:S(2)}, u32[]{:S(2)}) %collective-permute-start.1) | collective-permute-done | bytes 294944 | tf_op jit(solution)/shard_map/ppermute | solution.py:361
  68.9 6.0 %all-to-all-done.3.refs_0_ = bf16[8,128,256]{2,1,0:T(8,128)(2,1)S(1)} async-done(((bf16[8,128,256]{2,1,0:T(8,128)(2,1)}), bf16[8,128,256]{2,1,0:T(8,128)(2,1)S(1)}, u32[]{:S(2)}, u32[]{:S(2)}) %all-to-all-start.3) | async-done | bytes 524320 | tf_op jit(solution)/shard_map/all_to_all | solution.py:312
  74.9 2.4 %shard_map.104 = bf16[128,2048]{1,0:T(8,128)(2,1)} custom-call(bf16[8,128,256]{2,1,0:T(8,128)(2,1)S(1)} %all-to-all-done.3.refs_0_, bf16[128,512]{1,0:T(8,128)(2,1)S(1)} %copy-done.3, bf16[128,512]{1,0:T(8,128)(2,1)S(1)} %copy-done.4, s32[8,128]{1,0:T(8,128)S(1)} %broadcast_in_dim.2.refs_2_.refs_3_, bf16[144,1024]{1,0:T(8,128)(2,1)S(1)} %collective-permute-done.1.refs_4_, ...), custom_call_target="tpu_custom_call" | custom-call | tf_op jit(solution)/shard_map/pallas_call | solution.py:266
  (4 shorter events, 0.1 us)
Async XLA Ops:
  3.0 29.6 %copy-start.2 = (bf16[1024,256]{1,0:T(8,128)(2,1)S(1)}, bf16[1024,256]{1,0:T(8,128)(2,1)}, u32[]{:S(2)}) copy-start(bf16[1024,256]{1,0:T(8,128)(2,1)} %refs_2_.2) | copy-start | bytes 1572868
  15.3 17.3 %copy-start = (bf16[1024,256]{1,0:T(8,128)(2,1)S(1)}, bf16[1024,256]{1,0:T(8,128)(2,1)}, u32[]{:S(2)}) copy-start(bf16[1024,256]{1,0:T(8,128)(2,1)} %refs_1_.10) | copy-start | bytes 1572868
  15.3 17.3 %copy-start.1 = (bf16[1024,256]{1,0:T(8,128)(2,1)S(1)}, bf16[1024,256]{1,0:T(8,128)(2,1)}, u32[]{:S(2)}) copy-start(bf16[1024,256]{1,0:T(8,128)(2,1)} %refs_1_.6) | copy-start | bytes 1572868
  16.1 16.4 %copy-start.6 = (f32[16,2,11]{0,1,2:T(2,128)S(1)}, f32[16,2,11]{0,1,2:T(2,128)}, u32[]{:S(2)}) copy-start(f32[16,2,11]{0,1,2:T(2,128)} %param.12) | copy-start | bytes 4228
  16.1 29.9 %all-to-all-start.1 = ((bf16[4,272,128]{2,1,0:T(8,128)(2,1)}), bf16[4,272,128]{2,1,0:T(8,128)(2,1)S(1)}, u32[]{:S(2)}, u32[]{:S(2)}) async-start(bf16[4,272,128]{2,1,0:T(8,128)(2,1)} %shard_map.96.refs_5_), calls=%async_computation.1 | async-start | bytes 557056 | tf_op jit(solution)/shard_map/all_to_all | solution.py:312
  32.5 0.7 copy-start.5
  46.7 4.1 %copy-start.7 = (s32[128]{0:T(128)S(1)}, s32[128]{0:T(128)}, u32[]{:S(2)}) copy-start(s32[128]{0:T(128)} %param.15) | copy-start | bytes 1540
  46.7 4.1 %copy-start.3 = (bf16[128,512]{1,0:T(8,128)(2,1)S(1)}, bf16[128,512]{1,0:T(8,128)(2,1)}, u32[]{:S(2)}) copy-start(bf16[128,512]{1,0:T(8,128)(2,1)} %refs_1_.11) | copy-start | bytes 393220
  46.7 4.1 %copy-start.4 = (bf16[128,512]{1,0:T(8,128)(2,1)S(1)}, bf16[128,512]{1,0:T(8,128)(2,1)}, u32[]{:S(2)}) copy-start(bf16[128,512]{1,0:T(8,128)(2,1)} %refs_2_.3) | copy-start | bytes 393220
  46.7 9.8 %all-to-all-start.2 = ((bf16[4,272,128]{2,1,0:T(8,128)(2,1)}), bf16[4,272,128]{2,1,0:T(8,128)(2,1)S(1)}, u32[]{:S(2)}, u32[]{:S(2)}) async-start(bf16[4,272,128]{2,1,0:T(8,128)(2,1)} %shard_map.99.refs_3_), calls=%async_computation.2 | async-start | bytes 557056 | tf_op jit(solution)/shard_map/all_to_all | solution.py:312
  50.9 14.5 %collective-permute-start = (bf16[144,1024]{1,0:T(8,128)(2,1)S(1)}, bf16[144,1024]{1,0:T(8,128)(2,1)S(1)}, u32[]{:S(2)}, u32[]{:S(2)}) collective-permute-start(bf16[144,1024]{1,0:T(8,128)(2,1)S(1)} %shard_map.100.refs_5_.refs_0_), channel_id=1, source_target_pairs={{0,2},{1,3},{2,4},{3,5},{4,6},{5,7},{6,8},{7,9},{8,10},{9,11},{10,... | collective-permute-start | bytes 884744 | tf_op jit(solution)/shard_map/ppermute | solution.py:338
  58.8 16.1 %all-to-all-start.3 = ((bf16[8,128,256]{2,1,0:T(8,128)(2,1)}), bf16[8,128,256]{2,1,0:T(8,128)(2,1)S(1)}, u32[]{:S(2)}, u32[]{:S(2)}) async-start(bf16[8,128,256]{2,1,0:T(8,128)(2,1)} %get-tuple-element.5.refs_2_), calls=%async_computation.3 | async-start | bytes 1048576 | tf_op jit(solution)/shard_map/all_to_all | solution.py:312
  65.4 3.5 %collective-permute-start.1 = (bf16[144,1024]{1,0:T(8,128)(2,1)S(1)}, bf16[144,1024]{1,0:T(8,128)(2,1)S(1)}, u32[]{:S(2)}, u32[]{:S(2)}) collective-permute-start(bf16[144,1024]{1,0:T(8,128)(2,1)S(1)} %shard_map.103), channel_id=1, source_target_pairs={{0,1},{1,0},{2,3},{3,2},{4,5},{5,4},{6,7},{7,6},{8,9},{9,8},{10,11... | collective-permute-start | bytes 884744 | tf_op jit(solution)/shard_map/ppermute | solution.py:361

commit v5 on v4

--- a/solution.py
+++ b/solution.py
@@ -17,6 +17,7 @@
 TILE = 128
 CHUNK = 512
 PLAIN = (0, 1, 2, 3)
+HEAD_ORDER = (4, 0, 1, 2, 3, 5, 6, 7)
 ZL_ORDER = (1, 2, 0, 3)
 ZH_ORDER = (2, 0, 1, 3)
 CHUNKS = TOK // CHUNK
@@ -217,8 +218,8 @@
     def emit(rows, cols, acc):
         mixed = acc.astype(BF16)
         mixed_ref[rows, cols] = mixed
-        gate = 0.5 + 1.0 / (1.0 + jnp.exp(-mixed.astype(F32)))
-        gated_ref[rows.start // TILE, :, cols] = (q_ref[rows, cols].astype(F32) * gate).astype(BF16)
+        gate = 1.0 + 0.5 * jnp.tanh(0.5 * mixed.astype(F32))
+        gated_ref[HEAD_ORDER.index(rows.start // TILE), :, cols] = (q_ref[rows, cols].astype(F32) * gate).astype(BF16)
 
     two_levels(axis, order, first_lane, r_ref, q_ref, cls_ref, tab_ref, part_ref, emit)
 
@@ -247,7 +248,7 @@
         vals = jnp.concatenate([rim2_ref[:TILE, vcols], rim1_ref[:TILE, vcols], v_ref[:, cols]], axis=0)
         vals = jnp.concatenate([vals, ones], axis=1)
         for j in range(H // KVH):
-            src, part = 2 * g + j // 2, j % 2
+            src, part = HEAD_ORDER.index(2 * g + j // 2), j % 2
             sc = dot_nt(xq_ref[src, :, head_cols(part)], keys) * scale + bias
             top = jnp.max(sc, axis=1, keepdims=True)
             probs = jnp.exp2(sc - top).astype(BF16)
@@ -356,7 +357,7 @@
         tab,
         part,
     )
-    token_q = swap(gated, "head")
+    token_q = swap(gated, "head", HEAD_ORDER)
     picked = call(pick_kernel, rim, packed, rim2, after=(gated,))
     rim1 = lax.ppermute(picked, "head", [(i, i ^ 1) for i in range(8)])
     out = call(window_kernel, sds((TILE, H * E), BF16), token_q, win_keys, win_values, seg_rows, rim1, rim2)

time: 77.8 us -> 77.3 us (level)
  waiting for transfers between devices: 14.3 us -> 11.7 us
  starting transfers between devices: 32.3 us -> 34.4 us
    all_to_all x3, waiting for transfers between devices: 12.8 us -> 10.5 us  [swap(): lax.all_to_all(value, axis, split_axis=0, concat_axis=0, axis_index_group...]
    all_to_all x3, starting transfers between devices: 27.1 us -> 28.9 us  [swap(): lax.all_to_all(value, axis, split_axis=0, concat_axis=0, axis_index_group...]
where the time goes in v5:
time: 77.3 us; the launch traced here: 76.7 us
  starting transfers between devices  34.4 us (45%)
  Pallas kernels  16.8 us (22%)
  blocking collectives  12.3 us (16%)
  waiting for transfers between devices  11.7 us (15%)
    all_to_all x3, starting transfers between devices, swap(): lax.all_to_all(value, axis, split_axis=0, concat_axis=0, axis_index_group...  28.9 us
    pallas_call x9, Pallas kernels, call(): pl.pallas_call(body, out_shape=out, in_specs=[vmem] * count + [pl.BlockSp...  14.4 us
    all_to_all x1, blocking collectives, swap(): lax.all_to_all(value, axis, split_axis=0, concat_axis=0, axis_index_group...  12.3 us
    all_to_all x3, waiting for transfers between devices, swap(): lax.all_to_all(value, axis, split_axis=0, concat_axis=0, axis_index_group...  10.5 us
    ppermute x1, starting transfers between devices, local(): rim2 = lax.ppermute(packed, flat, [(i, i + 2) for i in range(510)])  3.22 us
    pallas_call x1, Pallas kernels, span_state(): pl.pallas_call(state_kernel, out_shape=jax.ShapeDtypeStruct((4, ROWS, E),...  2.35 us
    ppermute x1, starting transfers between devices, local(): rim1 = lax.ppermute(picked, 'head', [(i, i ^ 1) for i in range(8)])  2.27 us
  transfers between devices with their start and end apart: 5, of which 4 were waited for; matrix products, arithmetic and copies ran while one was open for 0% of the time, Pallas kernels for 14%

profile of v5, /device:TPU:1, one launch (start us, length us, event | category | flops | bytes accessed | tf_op | source)
XLA Modules:
  0.0 76.7 jit_solution(18148659493341888481)
XLA Ops:
  0.6 2.3 %shard_map.95 = bf16[4,272,128]{2,1,0:T(8,128)(2,1)} custom-call(bf16[1024,256]{1,0:T(8,128)(2,1)} %refs_1_.6, bf16[1024,256]{1,0:T(8,128)(2,1)} %refs_2_.2), custom_call_target="tpu_custom_call" | custom-call | tf_op jit(solution)/shard_map/pallas_call | solution.py:278
  3.0 0.0 copy-start.2
  3.0 12.3 %all_to_all.20.refs_0_ = bf16[4,272,128]{2,1,0:T(8,128)(2,1)S(1)} all-to-all(bf16[4,272,128]{2,1,0:T(8,128)(2,1)} %shard_map.95), channel_id=1, replica_groups={{8,16,0,24},{9,17,1,25},{10,18,2,26},{11,19,3,27},{12,20,4,28},{13,21,5..., dimensions={0} | all-to-all | bytes 557056 | tf_op jit(solution)/shard_map/all_to_all | solution.py:313
  15.3 0.0 copy-start
  15.3 0.0 copy-start.1
  15.3 0.8 shard_map.96.refs_5_
  16.1 0.0 copy-start.6
  16.1 16.4 %all-to-all-start.1 = ((bf16[4,272,128]{2,1,0:T(8,128)(2,1)}), bf16[4,272,128]{2,1,0:T(8,128)(2,1)S(1)}, u32[]{:S(2)}, u32[]{:S(2)}) async-start(bf16[4,272,128]{2,1,0:T(8,128)(2,1)} %shard_map.96.refs_5_), calls=%async_computation.1 | async-start | bytes 557056 | tf_op jit(solution)/shard_map/all_to_all | solution.py:313
  32.4 0.0 copy-done.6
  32.4 0.1 copy.12
  32.5 0.0 copy-start.5
  32.5 0.0 copy-done.2
  32.6 0.0 copy-done
  32.6 0.0 copy-done.1
  32.6 0.7 copy-done.5
  33.2 5.3 %shard_map.97.refs_4_ = f32[1024,256]{1,0:T(8,128)S(1)} custom-call(bf16[1024,256]{1,0:T(8,128)(2,1)S(1)} %copy-done, bf16[1024,256]{1,0:T(8,128)(2,1)S(1)} %copy-done.1, bf16[1024,256]{1,0:T(8,128)(2,1)S(1)} %copy-done.2, s32[8,128]{1,0:T(8,128)S(1)} %bitcast.2, f32[2,16,128]{2,1,0:T(8,128)S(1)} %pad.4.refs_4_.refs_3_, bf16[4,272,128]{2,1,0:T(8,128)(2,1)} %shard_map.96.refs_5_), custom_call_target="tpu_custom_call" | custom-call | tf_op jit(solution)/shard_map/pallas_call | solution.py:267
  38.5 1.5 %shard_map.98.refs_1_.refs_4_ = f32[1024,256]{1,0:T(8,128)S(1)} custom-call(bf16[4,272,128]{2,1,0:T(8,128)(2,1)S(1)} %all_to_all.20.refs_0_, bf16[1024,256]{1,0:T(8,128)(2,1)S(1)} %copy-done, s32[8,128]{1,0:T(8,128)S(1)} %bitcast.3, f32[2,16,128]{2,1,0:T(8,128)S(1)} %pad.4.refs_4_.refs_3_, ...), custom_call_target="tpu_custom_call", output_to_operand_aliasing={{}: (4, {})} | custom-call | tf_op jit(solution)/shard_map/pallas_call | solution.py:267
  40.0 5.9 %all-to-all-done.1.refs_0_ = bf16[4,272,128]{2,1,0:T(8,128)(2,1)S(1)} async-done(((bf16[4,272,128]{2,1,0:T(8,128)(2,1)}), bf16[4,272,128]{2,1,0:T(8,128)(2,1)S(1)}, u32[]{:S(2)}, u32[]{:S(2)}) %all-to-all-start.1) | async-done | bytes 278560 | tf_op jit(solution)/shard_map/all_to_all | solution.py:313
  46.0 0.8 shard_map.99.refs_3_
  46.7 0.0 copy-start.7
  46.7 0.0 copy-start.3
  46.7 0.0 copy-start.4
  46.7 4.1 %all-to-all-start.2 = ((bf16[4,272,128]{2,1,0:T(8,128)(2,1)}), bf16[4,272,128]{2,1,0:T(8,128)(2,1)S(1)}, u32[]{:S(2)}, u32[]{:S(2)}) async-start(bf16[4,272,128]{2,1,0:T(8,128)(2,1)} %shard_map.99.refs_3_), calls=%async_computation.2 | async-start | bytes 557056 | tf_op jit(solution)/shard_map/all_to_all | solution.py:313
  50.8 0.0 copy-done.7
  50.9 0.0 copy-done.3
  50.9 0.0 copy-done.4
  50.9 3.2 %collective-permute-start = (bf16[144,1024]{1,0:T(8,128)(2,1)S(1)}, bf16[144,1024]{1,0:T(8,128)(2,1)S(1)}, u32[]{:S(2)}, u32[]{:S(2)}) collective-permute-start(bf16[144,1024]{1,0:T(8,128)(2,1)S(1)} %shard_map.100.refs_5_.refs_0_), channel_id=1, source_target_pairs={{0,2},{1,3},{2,4},{3,5},{4,6},{5,7},{6,8},{7,9},{8,10},{9,11},{10,... | collective-permute-start | bytes 884744 | tf_op jit(solution)/shard_map/ppermute | solution.py:339
  54.1 1.5 %shard_map.101.refs_4_ = f32[1024,256]{1,0:T(8,128)S(1)} custom-call(bf16[4,272,128]{2,1,0:T(8,128)(2,1)S(1)} %all-to-all-done.1.refs_0_, bf16[1024,256]{1,0:T(8,128)(2,1)S(1)} %copy-done, s32[8,128]{1,0:T(8,128)S(1)} %bitcast.4, f32[2,16,128]{2,1,0:T(8,128)S(1)} %pad.4.refs_4_.refs_3_, ...), custom_call_target="tpu_custom_call", output_to_operand_aliasing={{}: (4, {})} | custom-call | tf_op jit(solution)/shard_map/pallas_call | solution.py:267
  55.6 0.9 %all-to-all-done.2.refs_0_ = bf16[4,272,128]{2,1,0:T(8,128)(2,1)S(1)} async-done(((bf16[4,272,128]{2,1,0:T(8,128)(2,1)}), bf16[4,272,128]{2,1,0:T(8,128)(2,1)S(1)}, u32[]{:S(2)}, u32[]{:S(2)}) %all-to-all-start.2) | async-done | bytes 278560 | tf_op jit(solution)/shard_map/all_to_all | solution.py:313
  56.5 2.2 %shard_map.102 = (bf16[1024,256]{1,0:T(8,128)(2,1)}, bf16[8,128,256]{2,1,0:T(8,128)(2,1)}) custom-call(bf16[4,272,128]{2,1,0:T(8,128)(2,1)S(1)} %all-to-all-done.2.refs_0_, bf16[1024,256]{1,0:T(8,128)(2,1)S(1)} %copy-done, s32[8,128]{1,0:T(8,128)S(1)} %bitcast.5, f32[2,16,128]{2,1,0:T(8,128)S(1)} %pad.4.refs_4_.refs_3_, f32[1024,256]{1,0:T(8,128)S(1)} %shard_map.101.refs_4_), custom_call_target="tpu_custom_call" | custom-call | tf_op jit(solution)/shard_map/pallas_call | solution.py:267
  58.7 8.4 %all-to-all-start.3 = ((bf16[8,128,256]{2,1,0:T(8,128)(2,1)}), bf16[8,128,256]{2,1,0:T(8,128)(2,1)S(1)}, u32[]{:S(2)}, u32[]{:S(2)}) async-start(bf16[8,128,256]{2,1,0:T(8,128)(2,1)} %get-tuple-element.5.refs_2_), calls=%async_computation.3 | async-start | bytes 1048576 | tf_op jit(solution)/shard_map/all_to_all | solution.py:313
  67.1 0.0 collective-permute-done.refs_1_.refs_5_
  67.1 2.3 %collective-permute-start.1 = (bf16[144,1024]{1,0:T(8,128)(2,1)S(1)}, bf16[144,1024]{1,0:T(8,128)(2,1)S(1)}, u32[]{:S(2)}, u32[]{:S(2)}) collective-permute-start(bf16[144,1024]{1,0:T(8,128)(2,1)S(1)} %shard_map.103), channel_id=1, source_target_pairs={{0,1},{1,0},{2,3},{3,2},{4,5},{5,4},{6,7},{7,6},{8,9},{9,8},{10,11... | collective-permute-start | bytes 884744 | tf_op jit(solution)/shard_map/ppermute | solution.py:362
  69.4 1.2 %collective-permute-done.1.refs_4_ = bf16[144,1024]{1,0:T(8,128)(2,1)S(1)} collective-permute-done((bf16[144,1024]{1,0:T(8,128)(2,1)S(1)}, bf16[144,1024]{1,0:T(8,128)(2,1)S(1)}, u32[]{:S(2)}, u32[]{:S(2)}) %collective-permute-start.1) | collective-permute-done | bytes 294944 | tf_op jit(solution)/shard_map/ppermute | solution.py:362
  70.6 3.7 %all-to-all-done.3.refs_0_ = bf16[8,128,256]{2,1,0:T(8,128)(2,1)S(1)} async-done(((bf16[8,128,256]{2,1,0:T(8,128)(2,1)}), bf16[8,128,256]{2,1,0:T(8,128)(2,1)S(1)}, u32[]{:S(2)}, u32[]{:S(2)}) %all-to-all-start.3) | async-done | bytes 524320 | tf_op jit(solution)/shard_map/all_to_all | solution.py:313
  74.3 2.4 %shard_map.104 = bf16[128,2048]{1,0:T(8,128)(2,1)} custom-call(bf16[8,128,256]{2,1,0:T(8,128)(2,1)S(1)} %all-to-all-done.3.refs_0_, bf16[128,512]{1,0:T(8,128)(2,1)S(1)} %copy-done.3, bf16[128,512]{1,0:T(8,128)(2,1)S(1)} %copy-done.4, s32[8,128]{1,0:T(8,128)S(1)} %broadcast_in_dim.2.refs_2_.refs_3_, bf16[144,1024]{1,0:T(8,128)(2,1)S(1)} %collective-permute-done.1.refs_4_, ...), custom_call_target="tpu_custom_call" | custom-call | tf_op jit(solution)/shard_map/pallas_call | solution.py:267
  (4 shorter events, 0.1 us)
Async XLA Ops:
  3.0 29.6 %copy-start.2 = (bf16[1024,256]{1,0:T(8,128)(2,1)S(1)}, bf16[1024,256]{1,0:T(8,128)(2,1)}, u32[]{:S(2)}) copy-start(bf16[1024,256]{1,0:T(8,128)(2,1)} %refs_2_.2) | copy-start | bytes 1572868
  15.3 17.3 %copy-start = (bf16[1024,256]{1,0:T(8,128)(2,1)S(1)}, bf16[1024,256]{1,0:T(8,128)(2,1)}, u32[]{:S(2)}) copy-start(bf16[1024,256]{1,0:T(8,128)(2,1)} %refs_1_.10) | copy-start | bytes 1572868
  15.3 17.3 %copy-start.1 = (bf16[1024,256]{1,0:T(8,128)(2,1)S(1)}, bf16[1024,256]{1,0:T(8,128)(2,1)}, u32[]{:S(2)}) copy-start(bf16[1024,256]{1,0:T(8,128)(2,1)} %refs_1_.6) | copy-start | bytes 1572868
  16.1 16.4 %copy-start.6 = (f32[16,2,11]{0,1,2:T(2,128)S(1)}, f32[16,2,11]{0,1,2:T(2,128)}, u32[]{:S(2)}) copy-start(f32[16,2,11]{0,1,2:T(2,128)} %param.12) | copy-start | bytes 4228
  16.1 29.9 %all-to-all-start.1 = ((bf16[4,272,128]{2,1,0:T(8,128)(2,1)}), bf16[4,272,128]{2,1,0:T(8,128)(2,1)S(1)}, u32[]{:S(2)}, u32[]{:S(2)}) async-start(bf16[4,272,128]{2,1,0:T(8,128)(2,1)} %shard_map.96.refs_5_), calls=%async_computation.1 | async-start | bytes 557056 | tf_op jit(solution)/shard_map/all_to_all | solution.py:313
  32.5 0.7 copy-start.5
  46.7 4.1 %copy-start.7 = (s32[128]{0:T(128)S(1)}, s32[128]{0:T(128)}, u32[]{:S(2)}) copy-start(s32[128]{0:T(128)} %param.15) | copy-start | bytes 1540
  46.7 4.1 %copy-start.3 = (bf16[128,512]{1,0:T(8,128)(2,1)S(1)}, bf16[128,512]{1,0:T(8,128)(2,1)}, u32[]{:S(2)}) copy-start(bf16[128,512]{1,0:T(8,128)(2,1)} %refs_1_.11) | copy-start | bytes 393220
  46.7 4.1 %copy-start.4 = (bf16[128,512]{1,0:T(8,128)(2,1)S(1)}, bf16[128,512]{1,0:T(8,128)(2,1)}, u32[]{:S(2)}) copy-start(bf16[128,512]{1,0:T(8,128)(2,1)} %refs_2_.3) | copy-start | bytes 393220
  46.7 9.8 %all-to-all-start.2 = ((bf16[4,272,128]{2,1,0:T(8,128)(2,1)}), bf16[4,272,128]{2,1,0:T(8,128)(2,1)S(1)}, u32[]{:S(2)}, u32[]{:S(2)}) async-start(bf16[4,272,128]{2,1,0:T(8,128)(2,1)} %shard_map.99.refs_3_), calls=%async_computation.2 | async-start | bytes 557056 | tf_op jit(solution)/shard_map/all_to_all | solution.py:313
  50.9 16.2 %collective-permute-start = (bf16[144,1024]{1,0:T(8,128)(2,1)S(1)}, bf16[144,1024]{1,0:T(8,128)(2,1)S(1)}, u32[]{:S(2)}, u32[]{:S(2)}) collective-permute-start(bf16[144,1024]{1,0:T(8,128)(2,1)S(1)} %shard_map.100.refs_5_.refs_0_), channel_id=1, source_target_pairs={{0,2},{1,3},{2,4},{3,5},{4,6},{5,7},{6,8},{7,9},{8,10},{9,11},{10,... | collective-permute-start | bytes 884744 | tf_op jit(solution)/shard_map/ppermute | solution.py:339
  58.7 15.6 %all-to-all-start.3 = ((bf16[8,128,256]{2,1,0:T(8,128)(2,1)}), bf16[8,128,256]{2,1,0:T(8,128)(2,1)S(1)}, u32[]{:S(2)}, u32[]{:S(2)}) async-start(bf16[8,128,256]{2,1,0:T(8,128)(2,1)} %get-tuple-element.5.refs_2_), calls=%async_computation.3 | async-start | bytes 1048576 | tf_op jit(solution)/shard_map/all_to_all | solution.py:313
  67.1 3.5 %collective-permute-start.1 = (bf16[144,1024]{1,0:T(8,128)(2,1)S(1)}, bf16[144,1024]{1,0:T(8,128)(2,1)S(1)}, u32[]{:S(2)}, u32[]{:S(2)}) collective-permute-start(bf16[144,1024]{1,0:T(8,128)(2,1)S(1)} %shard_map.103), channel_id=1, source_target_pairs={{0,1},{1,0},{2,3},{3,2},{4,5},{5,4},{6,7},{7,6},{8,9},{9,8},{10,11... | collective-permute-start | bytes 884744 | tf_op jit(solution)/shard_map/ppermute | solution.py:362

commit v6 on v5

--- a/solution.py
+++ b/solution.py
@@ -18,8 +18,8 @@
 CHUNK = 512
 PLAIN = (0, 1, 2, 3)
 HEAD_ORDER = (4, 0, 1, 2, 3, 5, 6, 7)
-ZL_ORDER = (1, 2, 0, 3)
-ZH_ORDER = (2, 0, 1, 3)
+ZL_ORDER = (2, 1, 0, 3)
+ZH_ORDER = (2, 0, 3, 1)
 CHUNKS = TOK // CHUNK
 SUMS = HEADS * E
 ROWS = SUMS + 16

time: 77.3 us -> 76 us (0.983)
  no operation moved by 1% of the time
where the time goes in v6:
time: 76 us; the launch traced here: 75.5 us
  starting transfers between devices  34.1 us (45%)
  Pallas kernels  16.8 us (22%)
  blocking collectives  12.1 us (16%)
  waiting for transfers between devices  11 us (14%)
  local copies, waits for them, and re-layouts  0.77 us (1%)
    all_to_all x3, starting transfers between devices, swap(): lax.all_to_all(value, axis, split_axis=0, concat_axis=0, axis_index_group...  28.6 us
    pallas_call x9, Pallas kernels, call(): pl.pallas_call(body, out_shape=out, in_specs=[vmem] * count + [pl.BlockSp...  14.4 us
    all_to_all x1, blocking collectives, swap(): lax.all_to_all(value, axis, split_axis=0, concat_axis=0, axis_index_group...  12.1 us
    all_to_all x3, waiting for transfers between devices, swap(): lax.all_to_all(value, axis, split_axis=0, concat_axis=0, axis_index_group...  9.78 us
    ppermute x1, starting transfers between devices, local(): rim2 = lax.ppermute(packed, flat, [(i, i + 2) for i in range(510)])  3.22 us
    pallas_call x1, Pallas kernels, span_state(): pl.pallas_call(state_kernel, out_shape=jax.ShapeDtypeStruct((4, ROWS, E),...  2.35 us
    ppermute x1, starting transfers between devices, local(): rim1 = lax.ppermute(picked, 'head', [(i, i ^ 1) for i in range(8)])  2.27 us
  transfers between devices with their start and end apart: 5, of which 4 were waited for; matrix products, arithmetic and copies ran while one was open for 0% of the time, Pallas kernels for 14%

profile of v6, /device:TPU:1, one launch (start us, length us, event | category | flops | bytes accessed | tf_op | source)
XLA Modules:
  0.0 75.5 jit_solution(13114305761545147479)
XLA Ops:
  0.6 2.3 %shard_map.95 = bf16[4,272,128]{2,1,0:T(8,128)(2,1)} custom-call(bf16[1024,256]{1,0:T(8,128)(2,1)} %refs_1_.6, bf16[1024,256]{1,0:T(8,128)(2,1)} %refs_2_.2), custom_call_target="tpu_custom_call" | custom-call | tf_op jit(solution)/shard_map/pallas_call | solution.py:278
  3.0 0.0 copy-start.2
  3.0 12.1 %all_to_all.20.refs_0_ = bf16[4,272,128]{2,1,0:T(8,128)(2,1)S(1)} all-to-all(bf16[4,272,128]{2,1,0:T(8,128)(2,1)} %shard_map.95), channel_id=1, replica_groups={{16,8,0,24},{17,9,1,25},{18,10,2,26},{19,11,3,27},{20,12,4,28},{21,13,5..., dimensions={0} | all-to-all | bytes 557056 | tf_op jit(solution)/shard_map/all_to_all | solution.py:313
  15.1 0.0 copy-start
  15.1 0.0 copy-start.1
  15.1 0.8 shard_map.96.refs_5_
  15.8 0.0 copy-start.6
  15.9 16.2 %all-to-all-start.1 = ((bf16[4,272,128]{2,1,0:T(8,128)(2,1)}), bf16[4,272,128]{2,1,0:T(8,128)(2,1)S(1)}, u32[]{:S(2)}, u32[]{:S(2)}) async-start(bf16[4,272,128]{2,1,0:T(8,128)(2,1)} %shard_map.96.refs_5_), calls=%async_computation.1 | async-start | bytes 557056 | tf_op jit(solution)/shard_map/all_to_all | solution.py:313
  32.1 0.0 copy-done.6
  32.1 0.1 copy.12
  32.2 0.0 copy-start.5
  32.2 0.0 copy-done.2
  32.2 0.0 copy-done
  32.2 0.0 copy-done.1
  32.2 0.7 copy-done.5
  32.9 5.3 %shard_map.97.refs_4_ = f32[1024,256]{1,0:T(8,128)S(1)} custom-call(bf16[1024,256]{1,0:T(8,128)(2,1)S(1)} %copy-done, bf16[1024,256]{1,0:T(8,128)(2,1)S(1)} %copy-done.1, bf16[1024,256]{1,0:T(8,128)(2,1)S(1)} %copy-done.2, s32[8,128]{1,0:T(8,128)S(1)} %bitcast.2, f32[2,16,128]{2,1,0:T(8,128)S(1)} %pad.4.refs_4_.refs_3_, bf16[4,272,128]{2,1,0:T(8,128)(2,1)} %shard_map.96.refs_5_), custom_call_target="tpu_custom_call" | custom-call | tf_op jit(solution)/shard_map/pallas_call | solution.py:267
  38.1 1.5 %shard_map.98.refs_1_.refs_4_ = f32[1024,256]{1,0:T(8,128)S(1)} custom-call(bf16[4,272,128]{2,1,0:T(8,128)(2,1)S(1)} %all_to_all.20.refs_0_, bf16[1024,256]{1,0:T(8,128)(2,1)S(1)} %copy-done, s32[8,128]{1,0:T(8,128)S(1)} %bitcast.3, f32[2,16,128]{2,1,0:T(8,128)S(1)} %pad.4.refs_4_.refs_3_, ...), custom_call_target="tpu_custom_call", output_to_operand_aliasing={{}: (4, {})} | custom-call | tf_op jit(solution)/shard_map/pallas_call | solution.py:267
  39.6 5.0 %all-to-all-done.1.refs_0_ = bf16[4,272,128]{2,1,0:T(8,128)(2,1)S(1)} async-done(((bf16[4,272,128]{2,1,0:T(8,128)(2,1)}), bf16[4,272,128]{2,1,0:T(8,128)(2,1)S(1)}, u32[]{:S(2)}, u32[]{:S(2)}) %all-to-all-start.1) | async-done | bytes 278560 | tf_op jit(solution)/shard_map/all_to_all | solution.py:313
  44.7 0.8 shard_map.99.refs_3_
  45.4 0.0 copy-start.7
  45.4 0.0 copy-start.3
  45.4 0.0 copy-start.4
  45.4 4.1 %all-to-all-start.2 = ((bf16[4,272,128]{2,1,0:T(8,128)(2,1)}), bf16[4,272,128]{2,1,0:T(8,128)(2,1)S(1)}, u32[]{:S(2)}, u32[]{:S(2)}) async-start(bf16[4,272,128]{2,1,0:T(8,128)(2,1)} %shard_map.99.refs_3_), calls=%async_computation.2 | async-start | bytes 557056 | tf_op jit(solution)/shard_map/all_to_all | solution.py:313
  49.6 0.0 copy-done.7
  49.6 0.0 copy-done.3
  49.6 0.0 copy-done.4
  49.6 3.2 %collective-permute-start = (bf16[144,1024]{1,0:T(8,128)(2,1)S(1)}, bf16[144,1024]{1,0:T(8,128)(2,1)S(1)}, u32[]{:S(2)}, u32[]{:S(2)}) collective-permute-start(bf16[144,1024]{1,0:T(8,128)(2,1)S(1)} %shard_map.100.refs_5_.refs_0_), channel_id=1, source_target_pairs={{0,2},{1,3},{2,4},{3,5},{4,6},{5,7},{6,8},{7,9},{8,10},{9,11},{10,... | collective-permute-start | bytes 884744 | tf_op jit(solution)/shard_map/ppermute | solution.py:339
  52.9 1.5 %shard_map.101.refs_4_ = f32[1024,256]{1,0:T(8,128)S(1)} custom-call(bf16[4,272,128]{2,1,0:T(8,128)(2,1)S(1)} %all-to-all-done.1.refs_0_, bf16[1024,256]{1,0:T(8,128)(2,1)S(1)} %copy-done, s32[8,128]{1,0:T(8,128)S(1)} %bitcast.4, f32[2,16,128]{2,1,0:T(8,128)S(1)} %pad.4.refs_4_.refs_3_, ...), custom_call_target="tpu_custom_call", output_to_operand_aliasing={{}: (4, {})} | custom-call | tf_op jit(solution)/shard_map/pallas_call | solution.py:267
  54.4 1.0 %all-to-all-done.2.refs_0_ = bf16[4,272,128]{2,1,0:T(8,128)(2,1)S(1)} async-done(((bf16[4,272,128]{2,1,0:T(8,128)(2,1)}), bf16[4,272,128]{2,1,0:T(8,128)(2,1)S(1)}, u32[]{:S(2)}, u32[]{:S(2)}) %all-to-all-start.2) | async-done | bytes 278560 | tf_op jit(solution)/shard_map/all_to_all | solution.py:313
  55.4 2.2 %shard_map.102 = (bf16[1024,256]{1,0:T(8,128)(2,1)}, bf16[8,128,256]{2,1,0:T(8,128)(2,1)}) custom-call(bf16[4,272,128]{2,1,0:T(8,128)(2,1)S(1)} %all-to-all-done.2.refs_0_, bf16[1024,256]{1,0:T(8,128)(2,1)S(1)} %copy-done, s32[8,128]{1,0:T(8,128)S(1)} %bitcast.5, f32[2,16,128]{2,1,0:T(8,128)S(1)} %pad.4.refs_4_.refs_3_, f32[1024,256]{1,0:T(8,128)S(1)} %shard_map.101.refs_4_), custom_call_target="tpu_custom_call" | custom-call | tf_op jit(solution)/shard_map/pallas_call | solution.py:267
  57.6 8.2 %all-to-all-start.3 = ((bf16[8,128,256]{2,1,0:T(8,128)(2,1)}), bf16[8,128,256]{2,1,0:T(8,128)(2,1)S(1)}, u32[]{:S(2)}, u32[]{:S(2)}) async-start(bf16[8,128,256]{2,1,0:T(8,128)(2,1)} %get-tuple-element.5.refs_2_), calls=%async_computation.3 | async-start | bytes 1048576 | tf_op jit(solution)/shard_map/all_to_all | solution.py:313
  65.8 0.0 collective-permute-done.refs_1_.refs_5_
  65.9 2.3 %collective-permute-start.1 = (bf16[144,1024]{1,0:T(8,128)(2,1)S(1)}, bf16[144,1024]{1,0:T(8,128)(2,1)S(1)}, u32[]{:S(2)}, u32[]{:S(2)}) collective-permute-start(bf16[144,1024]{1,0:T(8,128)(2,1)S(1)} %shard_map.103), channel_id=1, source_target_pairs={{0,1},{1,0},{2,3},{3,2},{4,5},{5,4},{6,7},{7,6},{8,9},{9,8},{10,11... | collective-permute-start | bytes 884744 | tf_op jit(solution)/shard_map/ppermute | solution.py:362
  68.1 1.2 %collective-permute-done.1.refs_4_ = bf16[144,1024]{1,0:T(8,128)(2,1)S(1)} collective-permute-done((bf16[144,1024]{1,0:T(8,128)(2,1)S(1)}, bf16[144,1024]{1,0:T(8,128)(2,1)S(1)}, u32[]{:S(2)}, u32[]{:S(2)}) %collective-permute-start.1) | collective-permute-done | bytes 294944 | tf_op jit(solution)/shard_map/ppermute | solution.py:362
  69.3 3.7 %all-to-all-done.3.refs_0_ = bf16[8,128,256]{2,1,0:T(8,128)(2,1)S(1)} async-done(((bf16[8,128,256]{2,1,0:T(8,128)(2,1)}), bf16[8,128,256]{2,1,0:T(8,128)(2,1)S(1)}, u32[]{:S(2)}, u32[]{:S(2)}) %all-to-all-start.3) | async-done | bytes 524320 | tf_op jit(solution)/shard_map/all_to_all | solution.py:313
  73.1 2.4 %shard_map.104 = bf16[128,2048]{1,0:T(8,128)(2,1)} custom-call(bf16[8,128,256]{2,1,0:T(8,128)(2,1)S(1)} %all-to-all-done.3.refs_0_, bf16[128,512]{1,0:T(8,128)(2,1)S(1)} %copy-done.3, bf16[128,512]{1,0:T(8,128)(2,1)S(1)} %copy-done.4, s32[8,128]{1,0:T(8,128)S(1)} %broadcast_in_dim.2.refs_2_.refs_3_, bf16[144,1024]{1,0:T(8,128)(2,1)S(1)} %collective-permute-done.1.refs_4_, ...), custom_call_target="tpu_custom_call" | custom-call | tf_op jit(solution)/shard_map/pallas_call | solution.py:267
  (4 shorter events, 0.1 us)
Async XLA Ops:
  3.0 29.2 %copy-start.2 = (bf16[1024,256]{1,0:T(8,128)(2,1)S(1)}, bf16[1024,256]{1,0:T(8,128)(2,1)}, u32[]{:S(2)}) copy-start(bf16[1024,256]{1,0:T(8,128)(2,1)} %refs_2_.2) | copy-start | bytes 1572868
  15.1 17.1 %copy-start = (bf16[1024,256]{1,0:T(8,128)(2,1)S(1)}, bf16[1024,256]{1,0:T(8,128)(2,1)}, u32[]{:S(2)}) copy-start(bf16[1024,256]{1,0:T(8,128)(2,1)} %refs_1_.10) | copy-start | bytes 1572868
  15.1 17.1 %copy-start.1 = (bf16[1024,256]{1,0:T(8,128)(2,1)S(1)}, bf16[1024,256]{1,0:T(8,128)(2,1)}, u32[]{:S(2)}) copy-start(bf16[1024,256]{1,0:T(8,128)(2,1)} %refs_1_.6) | copy-start | bytes 1572868
  15.8 16.2 %copy-start.6 = (f32[16,2,11]{0,1,2:T(2,128)S(1)}, f32[16,2,11]{0,1,2:T(2,128)}, u32[]{:S(2)}) copy-start(f32[16,2,11]{0,1,2:T(2,128)} %param.12) | copy-start | bytes 4228
  15.9 28.8 %all-to-all-start.1 = ((bf16[4,272,128]{2,1,0:T(8,128)(2,1)}), bf16[4,272,128]{2,1,0:T(8,128)(2,1)S(1)}, u32[]{:S(2)}, u32[]{:S(2)}) async-start(bf16[4,272,128]{2,1,0:T(8,128)(2,1)} %shard_map.96.refs_5_), calls=%async_computation.1 | async-start | bytes 557056 | tf_op jit(solution)/shard_map/all_to_all | solution.py:313
  32.2 0.7 copy-start.5
  45.4 4.2 %copy-start.7 = (s32[128]{0:T(128)S(1)}, s32[128]{0:T(128)}, u32[]{:S(2)}) copy-start(s32[128]{0:T(128)} %param.15) | copy-start | bytes 1540
  45.4 4.2 %copy-start.3 = (bf16[128,512]{1,0:T(8,128)(2,1)S(1)}, bf16[128,512]{1,0:T(8,128)(2,1)}, u32[]{:S(2)}) copy-start(bf16[128,512]{1,0:T(8,128)(2,1)} %refs_1_.11) | copy-start | bytes 393220
  45.4 4.2 %copy-start.4 = (bf16[128,512]{1,0:T(8,128)(2,1)S(1)}, bf16[128,512]{1,0:T(8,128)(2,1)}, u32[]{:S(2)}) copy-start(bf16[128,512]{1,0:T(8,128)(2,1)} %refs_2_.3) | copy-start | bytes 393220
  45.4 9.9 %all-to-all-start.2 = ((bf16[4,272,128]{2,1,0:T(8,128)(2,1)}), bf16[4,272,128]{2,1,0:T(8,128)(2,1)S(1)}, u32[]{:S(2)}, u32[]{:S(2)}) async-start(bf16[4,272,128]{2,1,0:T(8,128)(2,1)} %shard_map.99.refs_3_), calls=%async_computation.2 | async-start | bytes 557056 | tf_op jit(solution)/shard_map/all_to_all | solution.py:313
  49.6 16.2 %collective-permute-start = (bf16[144,1024]{1,0:T(8,128)(2,1)S(1)}, bf16[144,1024]{1,0:T(8,128)(2,1)S(1)}, u32[]{:S(2)}, u32[]{:S(2)}) collective-permute-start(bf16[144,1024]{1,0:T(8,128)(2,1)S(1)} %shard_map.100.refs_5_.refs_0_), channel_id=1, source_target_pairs={{0,2},{1,3},{2,4},{3,5},{4,6},{5,7},{6,8},{7,9},{8,10},{9,11},{10,... | collective-permute-start | bytes 884744 | tf_op jit(solution)/shard_map/ppermute | solution.py:339
  57.6 15.4 %all-to-all-start.3 = ((bf16[8,128,256]{2,1,0:T(8,128)(2,1)}), bf16[8,128,256]{2,1,0:T(8,128)(2,1)S(1)}, u32[]{:S(2)}, u32[]{:S(2)}) async-start(bf16[8,128,256]{2,1,0:T(8,128)(2,1)} %get-tuple-element.5.refs_2_), calls=%async_computation.3 | async-start | bytes 1048576 | tf_op jit(solution)/shard_map/all_to_all | solution.py:313
  65.9 3.5 %collective-permute-start.1 = (bf16[144,1024]{1,0:T(8,128)(2,1)S(1)}, bf16[144,1024]{1,0:T(8,128)(2,1)S(1)}, u32[]{:S(2)}, u32[]{:S(2)}) collective-permute-start(bf16[144,1024]{1,0:T(8,128)(2,1)S(1)} %shard_map.103), channel_id=1, source_target_pairs={{0,1},{1,0},{2,3},{3,2},{4,5},{5,4},{6,7},{7,6},{8,9},{9,8},{10,11... | collective-permute-start | bytes 884744 | tf_op jit(solution)/shard_map/ppermute | solution.py:362

commit v7 on v6

--- a/solution.py
+++ b/solution.py
@@ -18,7 +18,7 @@
 CHUNK = 512
 PLAIN = (0, 1, 2, 3)
 HEAD_ORDER = (4, 0, 1, 2, 3, 5, 6, 7)
-ZL_ORDER = (2, 1, 0, 3)
+ZL_ORDER = (2, 0, 3, 1)
 ZH_ORDER = (2, 0, 3, 1)
 CHUNKS = TOK // CHUNK
 SUMS = HEADS * E
@@ -224,7 +224,7 @@
     two_levels(axis, order, first_lane, r_ref, q_ref, cls_ref, tab_ref, part_ref, emit)
 
 
-def window_kernel(xq_ref, k_ref, v_ref, seg_ref, rim1_ref, rim2_ref, out_ref):
+def prepare_kernel(k_ref, v_ref, seg_ref, rim1_ref, rim2_ref, bias_ref, keys_ref, vals_ref):
     place = (
         (lax.axis_index("x") * 4 + lax.axis_index("zh")) * 4 + lax.axis_index("zl")
     ) * 8 + lax.axis_index("head")
@@ -235,18 +235,28 @@
     low = -1e30
     seg2 = rim2_ref[TILE : TILE + 1, :TILE].astype(F32)
     seg1 = rim1_ref[TILE : TILE + 1, :TILE].astype(F32)
-    bias2 = jnp.where((seg_q == seg2) & (s_col > t_row) & (place >= 2), 0.0, low)
-    bias1 = jnp.where((seg_q == seg1) & (place >= 1), 0.0, low)
-    bias0 = jnp.where((seg_q == seg_own) & (s_col <= t_row), 0.0, low)
-    bias = jnp.concatenate([bias2, bias1, bias0], axis=1)
-    scale = E ** (-0.5) * LOG2E
-    ones = jnp.ones((3 * TILE, E), BF16)
+    bias_ref[:, :TILE] = jnp.where((seg_q == seg2) & (s_col > t_row) & (place >= 2), 0.0, low)
+    bias_ref[:, TILE : 2 * TILE] = jnp.where((seg_q == seg1) & (place >= 1), 0.0, low)
+    bias_ref[:, 2 * TILE :] = jnp.where((seg_q == seg_own) & (s_col <= t_row), 0.0, low)
     for g in range(KVH):
         cols = slice(g * E, (g + 1) * E)
         vcols = slice((KVH + g) * E, (KVH + g + 1) * E)
-        keys = jnp.concatenate([rim2_ref[:TILE, cols], rim1_ref[:TILE, cols], k_ref[:, cols]], axis=0)
-        vals = jnp.concatenate([rim2_ref[:TILE, vcols], rim1_ref[:TILE, vcols], v_ref[:, cols]], axis=0)
-        vals = jnp.concatenate([vals, ones], axis=1)
+        keys_ref[g, :TILE] = rim2_ref[:TILE, cols]
+        keys_ref[g, TILE : 2 * TILE] = rim1_ref[:TILE, cols]
+        keys_ref[g, 2 * TILE :] = k_ref[:, cols]
+        vals_ref[g, :TILE, :E] = rim2_ref[:TILE, vcols]
+        vals_ref[g, TILE : 2 * TILE, :E] = rim1_ref[:TILE, vcols]
+        vals_ref[g, 2 * TILE :, :E] = v_ref[:, cols]
+        vals_ref[g, :, E:] = jnp.ones((3 * TILE, E), BF16)
+
+
+def window_kernel(xq_ref, bias_ref, keys_ref, vals_ref, out_hbm, out_ref, sems):
+    scale = E ** (-0.5) * LOG2E
+    bias = bias_ref[...]
+    copies = []
+    for g in range(KVH):
+        keys = keys_ref[g]
+        vals = vals_ref[g]
         for j in range(H // KVH):
             src, part = HEAD_ORDER.index(2 * g + j // 2), j % 2
             sc = dot_nt(xq_ref[src, :, head_cols(part)], keys) * scale + bias
@@ -255,6 +265,23 @@
             res = dot_nn(probs, vals)
             head = g * (H // KVH) + j
             out_ref[:, head_cols(head)] = (res[:, :E] / res[:, E:]).astype(BF16)
+        cols = slice(g * E * (H // KVH), (g + 1) * E * (H // KVH))
+        copies.append(pltpu.make_async_copy(out_ref.at[:, cols], out_hbm.at[:, cols], sems.at[g]))
+        copies[g].start()
+    for copy in copies:
+        copy.wait()
+
+
+def window(token_q, bias, keys, vals):
+    vmem = pl.BlockSpec(memory_space=pltpu.VMEM)
+    return pl.pallas_call(
+        window_kernel,
+        out_shape=jax.ShapeDtypeStruct((TILE, H * E), BF16),
+        in_specs=[vmem] * 4,
+        out_specs=pl.BlockSpec(memory_space=pltpu.HBM),
+        scratch_shapes=[pltpu.VMEM((TILE, H * E), BF16), pltpu.SemaphoreType.DMA((KVH,))],
+        compiler_params=pltpu.CompilerParams(vmem_limit_bytes=32 * 1024 * 1024),
+    )(token_q, bias, keys, vals)
 
 
 def call(kernel, out, *args, after=(), aliases=None):
@@ -331,10 +358,11 @@
         functools.partial(level_kernel, "zl", ZL_ORDER, 5), part_shape, from_zl, queries, cls, tab, part, aliases={4: 0}
     )
 
-    sum16 = call(total_kernel, copies, from_zh, after=(part,))
+    rim = sds((TILE + 16, 2 * KVH * E), BF16)
+    packed = call(pack_kernel, rim, win_keys, win_values, seg_rows, after=(sum4,))
+    sum16 = call(total_kernel, copies, from_zh, after=(part, packed))
     from_x = swap(sum16, "x")
-    rim = sds((TILE + 16, 2 * KVH * E), BF16)
-    packed = call(pack_kernel, rim, win_keys, win_values, seg_rows, after=(sum16,))
+    packed, sum16 = lax.optimization_barrier((packed, sum16))
     flat = ("x", "zh", "zl", "head")
     rim2 = lax.ppermute(packed, flat, [(i, i + 2) for i in range(510)])
     part = call(
@@ -345,7 +373,7 @@
         cls,
         tab,
         part,
-        after=(packed,),
+        after=(sum16,),
         aliases={4: 0},
     )
     mixed, gated = call(
@@ -360,8 +388,16 @@
     token_q = swap(gated, "head", HEAD_ORDER)
     picked = call(pick_kernel, rim, packed, rim2, after=(gated,))
     rim1 = lax.ppermute(picked, "head", [(i, i ^ 1) for i in range(8)])
-    out = call(window_kernel, sds((TILE, H * E), BF16), token_q, win_keys, win_values, seg_rows, rim1, rim2)
-    return mixed, out
+    laid = call(
+        prepare_kernel,
+        (sds((TILE, 3 * TILE), F32), sds((KVH, 3 * TILE, E), BF16), sds((KVH, 3 * TILE, 2 * E), BF16)),
+        win_keys,
+        win_values,
+        seg_rows,
+        rim1,
+        rim2,
+    )
+    return mixed, window(token_q, *laid)
 
 
 def solution(mesh):

time: 76 us -> 75.7 us (level)
    pallas_call x0 -> x1, Pallas kernels: none -> 2.36 us  [window(): pl.pallas_call(window_kernel, out_shape=jax.ShapeDtypeStruct((TILE, H * E...]
    pallas_call x9, Pallas kernels: 14.4 us -> 12.3 us  [call(): pl.pallas_call(body, out_shape=out, in_specs=[vmem] * count + [pl.BlockSp...]
where the time goes in v7:
time: 75.7 us; the launch traced here: 75.2 us
  starting transfers between devices  34.1 us (45%)
  Pallas kernels  17 us (22%)
  blocking collectives  12 us (16%)
  waiting for transfers between devices  10.3 us (14%)
  local copies, waits for them, and re-layouts  0.99 us (1%)
  between operations  0.77 us (1%)
    all_to_all x3, starting transfers between devices, swap(): lax.all_to_all(value, axis, split_axis=0, concat_axis=0, axis_index_group...  28.5 us
    pallas_call x9, Pallas kernels, call(): pl.pallas_call(body, out_shape=out, in_specs=[vmem] * count + [pl.BlockSp...  12.3 us
    all_to_all x1, blocking collectives, swap(): lax.all_to_all(value, axis, split_axis=0, concat_axis=0, axis_index_group...  12 us
    all_to_all x3, waiting for transfers between devices, swap(): lax.all_to_all(value, axis, split_axis=0, concat_axis=0, axis_index_group...  9.08 us
    ppermute x1, starting transfers between devices, local(): rim2 = lax.ppermute(packed, flat, [(i, i + 2) for i in range(510)])  3.21 us
    ppermute x1, starting transfers between devices, local(): rim1 = lax.ppermute(picked, 'head', [(i, i ^ 1) for i in range(8)])  2.4 us
    pallas_call x1, Pallas kernels, window(): pl.pallas_call(window_kernel, out_shape=jax.ShapeDtypeStruct((TILE, H * E...  2.36 us
    pallas_call x1, Pallas kernels, span_state(): pl.pallas_call(state_kernel, out_shape=jax.ShapeDtypeStruct((4, ROWS, E),...  2.35 us
  transfers between devices with their start and end apart: 5, of which 4 were waited for; matrix products, arithmetic and copies ran while one was open for 0% of the time, Pallas kernels for 14%

profile of v7, /device:TPU:1, one launch (start us, length us, event | category | flops | bytes accessed | tf_op | source)
XLA Modules:
  0.0 75.2 jit_solution(11793138802306887954)
XLA Ops:
  0.6 2.3 %shard_map.95 = bf16[4,272,128]{2,1,0:T(8,128)(2,1)} custom-call(bf16[1024,256]{1,0:T(8,128)(2,1)} %refs_1_.6, bf16[1024,256]{1,0:T(8,128)(2,1)} %refs_2_.1), custom_call_target="tpu_custom_call" | custom-call | tf_op jit(solution)/shard_map/pallas_call | solution.py:305
  3.0 12.0 %all_to_all.20.refs_0_ = bf16[4,272,128]{2,1,0:T(8,128)(2,1)S(1)} all-to-all(bf16[4,272,128]{2,1,0:T(8,128)(2,1)} %shard_map.95), channel_id=1, replica_groups={{16,0,24,8},{17,1,25,9},{18,2,26,10},{19,3,27,11},{20,4,28,12},{21,5,29..., dimensions={0} | all-to-all | bytes 557056 | tf_op jit(solution)/shard_map/all_to_all | solution.py:340
  14.9 0.0 copy-start.8
  14.9 0.0 copy-start.9
  15.0 0.0 copy-start.3
  15.0 0.0 copy-start.5
  15.0 0.0 copy-start.2
  15.0 0.8 %shard_map.96.refs_5_.refs_3_ = bf16[4,272,128]{2,1,0:T(8,128)(2,1)} custom-call(bf16[4,272,128]{2,1,0:T(8,128)(2,1)S(1)} %all_to_all.20.refs_0_), custom_call_target="tpu_custom_call" | custom-call | tf_op jit(solution)/shard_map/pallas_call | solution.py:294
  15.7 0.0 copy-start.1
  15.7 16.1 %all-to-all-start.1 = ((bf16[4,272,128]{2,1,0:T(8,128)(2,1)}), bf16[4,272,128]{2,1,0:T(8,128)(2,1)S(1)}, u32[]{:S(2)}, u32[]{:S(2)}) async-start(bf16[4,272,128]{2,1,0:T(8,128)(2,1)} %shard_map.96.refs_5_.refs_3_), calls=%async_computation.1 | async-start | bytes 557056 | tf_op jit(solution)/shard_map/all_to_all | solution.py:340
  31.9 0.0 copy-done.8
  31.9 0.0 copy-start
  31.9 0.1 copy.12
  32.0 0.0 copy-done.9
  32.0 0.0 copy-done.3
  32.0 0.0 copy-done.5
  32.0 0.0 copy-start.7
  32.0 0.0 copy-done.2
  32.1 0.0 copy-done.1
  32.1 0.9 %copy-done = bf16[1024,256]{1,0:T(8,128)(2,1)S(1)} copy-done((bf16[1024,256]{1,0:T(8,128)(2,1)S(1)}, bf16[1024,256]{1,0:T(8,128)(2,1)}, u32[]{:S(2)}) %copy-start) | copy-done | bytes 524312
  32.9 0.0 copy-done.7
  32.9 5.3 %shard_map.97.refs_4_ = f32[1024,256]{1,0:T(8,128)S(1)} custom-call(bf16[1024,256]{1,0:T(8,128)(2,1)S(1)} %copy-done, bf16[1024,256]{1,0:T(8,128)(2,1)S(1)} %copy-done.1, bf16[1024,256]{1,0:T(8,128)(2,1)S(1)} %copy-done.2, s32[8,128]{1,0:T(8,128)S(1)} %bitcast.2, f32[2,16,128]{2,1,0:T(8,128)S(1)} %pad.4.refs_4_.refs_3_, ...), custom_call_target="tpu_custom_call" | custom-call | tf_op jit(solution)/shard_map/pallas_call | solution.py:294
  38.2 1.5 %shard_map.98.refs_1_.refs_4_ = f32[1024,256]{1,0:T(8,128)S(1)} custom-call(bf16[4,272,128]{2,1,0:T(8,128)(2,1)S(1)} %all_to_all.20.refs_0_, bf16[1024,256]{1,0:T(8,128)(2,1)S(1)} %copy-done, s32[8,128]{1,0:T(8,128)S(1)} %bitcast.3, f32[2,16,128]{2,1,0:T(8,128)S(1)} %pad.4.refs_4_.refs_3_, ...), custom_call_target="tpu_custom_call", output_to_operand_aliasing={{}: (4, {})} | custom-call | tf_op jit(solution)/shard_map/pallas_call | solution.py:294
  39.7 4.8 %all-to-all-done.1.refs_0_ = bf16[4,272,128]{2,1,0:T(8,128)(2,1)S(1)} async-done(((bf16[4,272,128]{2,1,0:T(8,128)(2,1)}), bf16[4,272,128]{2,1,0:T(8,128)(2,1)S(1)}, u32[]{:S(2)}, u32[]{:S(2)}) %all-to-all-start.1) | async-done | bytes 278560 | tf_op jit(solution)/shard_map/all_to_all | solution.py:340
  44.5 0.8 %shard_map.100.refs_5_ = bf16[4,272,128]{2,1,0:T(8,128)(2,1)} custom-call(bf16[4,272,128]{2,1,0:T(8,128)(2,1)S(1)} %all-to-all-done.1.refs_0_, f32[1024,256]{1,0:T(8,128)S(1)} %shard_map.98.refs_1_.refs_4_, bf16[144,1024]{1,0:T(8,128)(2,1)S(1)} %shard_map.99.refs_2_.refs_0_), custom_call_target="tpu_custom_call" | custom-call | tf_op jit(solution)/shard_map/pallas_call | solution.py:294
  45.3 4.0 %all-to-all-start.2 = ((bf16[4,272,128]{2,1,0:T(8,128)(2,1)}), bf16[4,272,128]{2,1,0:T(8,128)(2,1)S(1)}, u32[]{:S(2)}, u32[]{:S(2)}) async-start(bf16[4,272,128]{2,1,0:T(8,128)(2,1)} %shard_map.100.refs_5_), calls=%async_computation.2 | async-start | bytes 557056 | tf_op jit(solution)/shard_map/all_to_all | solution.py:340
  49.3 3.2 %collective-permute-start = (bf16[144,1024]{1,0:T(8,128)(2,1)S(1)}, bf16[144,1024]{1,0:T(8,128)(2,1)S(1)}, u32[]{:S(2)}, u32[]{:S(2)}) collective-permute-start(bf16[144,1024]{1,0:T(8,128)(2,1)S(1)} %shard_map.99.refs_2_.refs_0_), channel_id=1, source_target_pairs={{0,2},{1,3},{2,4},{3,5},{4,6},{5,7},{6,8},{7,9},{8,10},{9,11},{10,... | collective-permute-start | bytes 884744 | tf_op jit(solution)/shard_map/ppermute | solution.py:367
  52.5 1.5 %shard_map.101.refs_4_ = f32[1024,256]{1,0:T(8,128)S(1)} custom-call(bf16[4,272,128]{2,1,0:T(8,128)(2,1)S(1)} %all-to-all-done.1.refs_0_, bf16[1024,256]{1,0:T(8,128)(2,1)S(1)} %copy-done, s32[8,128]{1,0:T(8,128)S(1)} %bitcast.4, f32[2,16,128]{2,1,0:T(8,128)S(1)} %pad.4.refs_4_.refs_3_, ...), custom_call_target="tpu_custom_call", output_to_operand_aliasing={{}: (4, {})} | custom-call | tf_op jit(solution)/shard_map/pallas_call | solution.py:294
  54.0 0.9 %all-to-all-done.2.refs_0_ = bf16[4,272,128]{2,1,0:T(8,128)(2,1)S(1)} async-done(((bf16[4,272,128]{2,1,0:T(8,128)(2,1)}), bf16[4,272,128]{2,1,0:T(8,128)(2,1)S(1)}, u32[]{:S(2)}, u32[]{:S(2)}) %all-to-all-start.2) | async-done | bytes 278560 | tf_op jit(solution)/shard_map/all_to_all | solution.py:340
  55.0 2.2 %shard_map.102 = (bf16[1024,256]{1,0:T(8,128)(2,1)}, bf16[8,128,256]{2,1,0:T(8,128)(2,1)}) custom-call(bf16[4,272,128]{2,1,0:T(8,128)(2,1)S(1)} %all-to-all-done.2.refs_0_, bf16[1024,256]{1,0:T(8,128)(2,1)S(1)} %copy-done, s32[8,128]{1,0:T(8,128)S(1)} %bitcast.5, f32[2,16,128]{2,1,0:T(8,128)S(1)} %pad.4.refs_4_.refs_3_, f32[1024,256]{1,0:T(8,128)S(1)} %shard_map.101.refs_4_), custom_call_target="tpu_custom_call" | custom-call | tf_op jit(solution)/shard_map/pallas_call | solution.py:294
  57.2 8.4 %all-to-all-start.3 = ((bf16[8,128,256]{2,1,0:T(8,128)(2,1)}), bf16[8,128,256]{2,1,0:T(8,128)(2,1)S(1)}, u32[]{:S(2)}, u32[]{:S(2)}) async-start(bf16[8,128,256]{2,1,0:T(8,128)(2,1)} %get-tuple-element.11.refs_2_), calls=%async_computation.3 | async-start | bytes 1048576 | tf_op jit(solution)/shard_map/all_to_all | solution.py:340
  65.6 0.0 copy-start.4
  65.6 0.0 copy-start.6
  65.6 0.0 collective-permute-done.refs_1_.refs_4_
  65.6 2.4 %collective-permute-start.1 = (bf16[144,1024]{1,0:T(8,128)(2,1)S(1)}, bf16[144,1024]{1,0:T(8,128)(2,1)S(1)}, u32[]{:S(2)}, u32[]{:S(2)}) collective-permute-start(bf16[144,1024]{1,0:T(8,128)(2,1)S(1)} %shard_map.103), channel_id=1, source_target_pairs={{0,1},{1,0},{2,3},{3,2},{4,5},{5,4},{6,7},{7,6},{8,9},{9,8},{10,11... | collective-permute-start | bytes 884744 | tf_op jit(solution)/shard_map/ppermute | solution.py:390
  68.0 1.2 %collective-permute-done.1.refs_3_ = bf16[144,1024]{1,0:T(8,128)(2,1)S(1)} collective-permute-done((bf16[144,1024]{1,0:T(8,128)(2,1)S(1)}, bf16[144,1024]{1,0:T(8,128)(2,1)S(1)}, u32[]{:S(2)}, u32[]{:S(2)}) %collective-permute-start.1) | collective-permute-done | bytes 294944 | tf_op jit(solution)/shard_map/ppermute | solution.py:390
  69.2 0.0 copy-done.4
  69.2 0.0 copy-done.6
  69.2 0.2 shard_map.104
  69.5 3.3 %all-to-all-done.3.xq_ref = bf16[8,128,256]{2,1,0:T(8,128)(2,1)S(1)} async-done(((bf16[8,128,256]{2,1,0:T(8,128)(2,1)}), bf16[8,128,256]{2,1,0:T(8,128)(2,1)S(1)}, u32[]{:S(2)}, u32[]{:S(2)}) %all-to-all-start.3) | async-done | bytes 524320 | tf_op jit(solution)/shard_map/all_to_all | solution.py:340
  72.8 2.4 %shard_map.105 = bf16[128,2048]{1,0:T(8,128)(2,1)} custom-call(bf16[8,128,256]{2,1,0:T(8,128)(2,1)S(1)} %all-to-all-done.3.xq_ref, f32[128,384]{1,0:T(8,128)S(1)} %get-tuple-element.13.bias_ref, bf16[4,384,128]{2,1,0:T(8,128)(2,1)S(1)} %get-tuple-element.14.keys_ref, bf16[4,384,256]{2,1,0:T(8,128)(2,1)S(1)} %get-tuple-element.15.vals_ref), custom_call_target="tpu_custom_call" | custom-call | tf_op jit(solution)/shard_map/pallas_call | solution.py:277
  (4 shorter events, 0.1 us)
Async XLA Ops:
  14.9 16.9 %copy-start.8 = (f32[16,2,11]{0,1,2:T(2,128)S(1)}, f32[16,2,11]{0,1,2:T(2,128)}, u32[]{:S(2)}) copy-start(f32[16,2,11]{0,1,2:T(2,128)} %param.12) | copy-start | bytes 4228
  14.9 17.0 %copy-start.9 = (s32[128]{0:T(128)S(1)}, s32[128]{0:T(128)}, u32[]{:S(2)}) copy-start(s32[128]{0:T(128)} %param.15) | copy-start | bytes 1540
  15.0 17.0 %copy-start.3 = (bf16[128,512]{1,0:T(8,128)(2,1)S(1)}, bf16[128,512]{1,0:T(8,128)(2,1)}, u32[]{:S(2)}) copy-start(bf16[128,512]{1,0:T(8,128)(2,1)} %refs_0_.5) | copy-start | bytes 393220
  15.0 17.0 %copy-start.5 = (bf16[128,512]{1,0:T(8,128)(2,1)S(1)}, bf16[128,512]{1,0:T(8,128)(2,1)}, u32[]{:S(2)}) copy-start(bf16[128,512]{1,0:T(8,128)(2,1)} %refs_1_.11) | copy-start | bytes 393220
  15.0 17.1 %copy-start.2 = (bf16[1024,256]{1,0:T(8,128)(2,1)S(1)}, bf16[1024,256]{1,0:T(8,128)(2,1)}, u32[]{:S(2)}) copy-start(bf16[1024,256]{1,0:T(8,128)(2,1)} %refs_2_.1) | copy-start | bytes 1572868
  15.7 16.3 %copy-start.1 = (bf16[1024,256]{1,0:T(8,128)(2,1)S(1)}, bf16[1024,256]{1,0:T(8,128)(2,1)}, u32[]{:S(2)}) copy-start(bf16[1024,256]{1,0:T(8,128)(2,1)} %refs_1_.6) | copy-start | bytes 1572868
  15.7 28.8 %all-to-all-start.1 = ((bf16[4,272,128]{2,1,0:T(8,128)(2,1)}), bf16[4,272,128]{2,1,0:T(8,128)(2,1)S(1)}, u32[]{:S(2)}, u32[]{:S(2)}) async-start(bf16[4,272,128]{2,1,0:T(8,128)(2,1)} %shard_map.96.refs_5_.refs_3_), calls=%async_computation.1 | async-start | bytes 557056 | tf_op jit(solution)/shard_map/all_to_all | solution.py:340
  31.9 1.0 %copy-start = (bf16[1024,256]{1,0:T(8,128)(2,1)S(1)}, bf16[1024,256]{1,0:T(8,128)(2,1)}, u32[]{:S(2)}) copy-start(bf16[1024,256]{1,0:T(8,128)(2,1)} %refs_1_.10) | copy-start | bytes 1572868
  32.0 0.9 %copy-start.7 = (s32[1024]{0:T(1024)S(1)}, s32[1024]{0:T(1024)}, u32[]{:S(2)}) copy-start(s32[1024]{0:T(1024)} %param.11) | copy-start | bytes 12292
  45.3 9.7 %all-to-all-start.2 = ((bf16[4,272,128]{2,1,0:T(8,128)(2,1)}), bf16[4,272,128]{2,1,0:T(8,128)(2,1)S(1)}, u32[]{:S(2)}, u32[]{:S(2)}) async-start(bf16[4,272,128]{2,1,0:T(8,128)(2,1)} %shard_map.100.refs_5_), calls=%async_computation.2 | async-start | bytes 557056 | tf_op jit(solution)/shard_map/all_to_all | solution.py:340
  49.3 16.3 %collective-permute-start = (bf16[144,1024]{1,0:T(8,128)(2,1)S(1)}, bf16[144,1024]{1,0:T(8,128)(2,1)S(1)}, u32[]{:S(2)}, u32[]{:S(2)}) collective-permute-start(bf16[144,1024]{1,0:T(8,128)(2,1)S(1)} %shard_map.99.refs_2_.refs_0_), channel_id=1, source_target_pairs={{0,2},{1,3},{2,4},{3,5},{4,6},{5,7},{6,8},{7,9},{8,10},{9,11},{10,... | collective-permute-start | bytes 884744 | tf_op jit(solution)/shard_map/ppermute | solution.py:367
  57.2 15.6 %all-to-all-start.3 = ((bf16[8,128,256]{2,1,0:T(8,128)(2,1)}), bf16[8,128,256]{2,1,0:T(8,128)(2,1)S(1)}, u32[]{:S(2)}, u32[]{:S(2)}) async-start(bf16[8,128,256]{2,1,0:T(8,128)(2,1)} %get-tuple-element.11.refs_2_), calls=%async_computation.3 | async-start | bytes 1048576 | tf_op jit(solution)/shard_map/all_to_all | solution.py:340
  65.6 3.7 %copy-start.4 = (bf16[128,512]{1,0:T(8,128)(2,1)S(1)}, bf16[128,512]{1,0:T(8,128)(2,1)}, u32[]{:S(2)}) copy-start(bf16[128,512]{1,0:T(8,128)(2,1)} %refs_0_.5) | copy-start | bytes 393220
  65.6 3.7 %copy-start.6 = (bf16[128,512]{1,0:T(8,128)(2,1)S(1)}, bf16[128,512]{1,0:T(8,128)(2,1)}, u32[]{:S(2)}) copy-start(bf16[128,512]{1,0:T(8,128)(2,1)} %refs_1_.11) | copy-start | bytes 393220
  65.6 3.6 %collective-permute-start.1 = (bf16[144,1024]{1,0:T(8,128)(2,1)S(1)}, bf16[144,1024]{1,0:T(8,128)(2,1)S(1)}, u32[]{:S(2)}, u32[]{:S(2)}) collective-permute-start(bf16[144,1024]{1,0:T(8,128)(2,1)S(1)} %shard_map.103), channel_id=1, source_target_pairs={{0,1},{1,0},{2,3},{3,2},{4,5},{5,4},{6,7},{7,6},{8,9},{9,8},{10,11... | collective-permute-start | bytes 884744 | tf_op jit(solution)/shard_map/ppermute | solution.py:390
